TPU v7x, 128 devices: a whole 4x4x4 slice. The times are simulated.
128 devices in a mesh: rows: 64 (over y, x, z), chan: 2 (over core).
Axes of the slice: x: 4, y: 4, z: 4, core: 2. Of those that a mesh axis runs over, the one named last changes fastest.
Arguments:
- field: bfloat16 [32, 1024, 4096], P('chan', 'rows'), may hold values from -6 to 6
- spec_weight: float32 [2, 2, 32, 32, 128, 128], P(None, None, 'chan', None, 'rows'), may hold values from -0.75 to 0.75
- conv_weight: bfloat16 [2, 2, 3, 3, 16, 16], P(None, 'chan'), may hold values from -0.5 to 0.5
- bias: float32 [2, 32], P(None, 'chan'), may hold values from -4 to 4
Outputs:
- output_field: bfloat16 [32, 1024, 4096], P('chan', 'rows')
All inputs are finite; a program needn't handle non-finite values.
Results may differ from a plain program's by a relative error of at most 0.024.
Values may be sent and summed in bfloat16 or wider, within the bound.
A program may use at most 128 MiB of HBM per device.

v0:
```python
import math

import jax
import jax.numpy as jnp
from jax import lax
from jax.sharding import PartitionSpec as P

M = 128
LAYERS = 2


TWO_PI = 2.0 * math.pi


def padded_2(block, sides, width):
    for axis, dim in sides:
        count = lax.axis_size(axis)
        forward = [(i, i + 1) for i in range(count - 1)]
        backward = [(target, source) for source, target in forward]
        low = lax.ppermute(
            lax.slice_in_dim(block, block.shape[dim] - width, None, axis=dim), axis, forward
        )
        high = lax.ppermute(lax.slice_in_dim(block, 0, width, axis=dim), axis, backward)
        block = jnp.concatenate([low, block, high], axis=dim)
    return block


def phase_angles(count, first, freqs, length):
    positions = first + jnp.arange(count, dtype=jnp.int32)
    products = positions[:, None] * freqs[None, :] % length
    return products.astype(jnp.float32) * (TWO_PI / length)


def forward_table(columns, modes):
    angles = phase_angles(columns, 0, jnp.arange(modes, dtype=jnp.int32), columns)
    return (
        jnp.stack([jnp.cos(angles), -jnp.sin(angles)], axis=2)
        .reshape(columns, 2 * modes)
        .astype(jnp.bfloat16)
    )


def backward_table(columns, modes):
    orders = jnp.arange(modes, dtype=jnp.int32)
    angles = phase_angles(columns, 0, orders, columns)
    factor = jnp.where(orders == 0, 1.0, 2.0).astype(jnp.float32) / modes
    cosine = jnp.cos(angles).T * factor[:, None]
    sine = jnp.sin(angles).T * factor[:, None]
    return jnp.stack([cosine, -sine], axis=1).reshape(2 * modes, columns).astype(jnp.bfloat16)


def row_tables(count, first, all_rows, modes):
    indices = jnp.arange(modes, dtype=jnp.int32)
    freqs = jnp.where(indices < modes // 2, indices, all_rows - modes + indices)
    angles = phase_angles(count, first, freqs, all_rows)
    return (jnp.cos(angles).astype(jnp.bfloat16), jnp.sin(angles).astype(jnp.bfloat16))


def forward_rows(pairs, cosine, sine):
    shaped = pairs.reshape(pairs.shape[0] // 2, 2, pairs.shape[1], pairs.shape[2])
    real_part = shaped[:, 0]
    imag_part = shaped[:, 1]
    mode_real = jnp.einsum(
        "ycx,xk->yck", real_part, cosine, preferred_element_type=jnp.float32
    ) + jnp.einsum("ycx,xk->yck", imag_part, sine, preferred_element_type=jnp.float32)
    mode_imag = jnp.einsum(
        "ycx,xk->yck", imag_part, cosine, preferred_element_type=jnp.float32
    ) - jnp.einsum("ycx,xk->yck", real_part, sine, preferred_element_type=jnp.float32)
    stacked = jnp.stack([mode_real, mode_imag], axis=1)
    return stacked.reshape(pairs.shape[0], pairs.shape[1], cosine.shape[1])


def mix_modes(modes_arr, weight):
    shaped = modes_arr.reshape(modes_arr.shape[0] // 2, 2, modes_arr.shape[1], modes_arr.shape[2])
    mode_real = jnp.transpose(shaped[:, 0], (1, 0, 2))[:, None]
    mode_imag = jnp.transpose(shaped[:, 1], (1, 0, 2))[:, None]
    mixed_real = jnp.sum(weight[0] * mode_real - weight[1] * mode_imag, axis=0)
    mixed_imag = jnp.sum(weight[0] * mode_imag + weight[1] * mode_real, axis=0)
    return (mixed_real, mixed_imag)


def back_rows(mixed_real, mixed_imag, cosine, sine):
    back_real = jnp.einsum(
        "oyk,xk->yox", mixed_real, cosine, preferred_element_type=jnp.float32
    ) - jnp.einsum("oyk,xk->yox", mixed_imag, sine, preferred_element_type=jnp.float32)
    back_imag = jnp.einsum(
        "oyk,xk->yox", mixed_real, sine, preferred_element_type=jnp.float32
    ) + jnp.einsum("oyk,xk->yox", mixed_imag, cosine, preferred_element_type=jnp.float32)
    stacked = jnp.stack([back_real, back_imag], axis=1)
    return stacked.reshape(2 * mixed_real.shape[1], mixed_real.shape[0], cosine.shape[0]).astype(
        jnp.bfloat16
    )


def local_conv(padded, taps):
    height = padded.shape[1] - 2
    width = padded.shape[2] - 2
    total = jnp.zeros((taps.shape[2], height, width), jnp.float32)
    for row_off in range(3):
        for col_off in range(3):
            window = padded[:, row_off : row_off + height, col_off : col_off + width]
            total = total + lax.dot_general(
                taps[row_off, col_off],
                window,
                (((1,), (0,)), ((), ())),
                preferred_element_type=jnp.float32,
            )
    return total


def body(field, spec_weight, conv_weight, bias):
    group_width, slab_rows, columns = field.shape
    row_devices = lax.axis_size("rows")
    all_rows = slab_rows * row_devices
    fwd_table = forward_table(columns, M)
    bwd_table = backward_table(columns, M)
    cosine, sine = row_tables(all_rows, 0, all_rows, M)
    scale = 1.0 / math.sqrt(all_rows * columns)
    hidden_field = field
    for layer in range(LAYERS):
        row_sums = lax.dot_general(
            fwd_table, hidden_field, (((0,), (2,)), ((), ())), preferred_element_type=jnp.float32
        )
        row_modes = (row_sums * scale).astype(jnp.bfloat16)
        mode_part = forward_rows(
            lax.all_to_all(row_modes, "rows", split_axis=0, concat_axis=2, tiled=True), cosine, sine
        )
        part_real, part_imag = mix_modes(mode_part, spec_weight[layer])
        summed_real, summed_imag = (
            lax.psum_scatter(
                part_real.astype(jnp.bfloat16), "chan", scatter_dimension=0, tiled=True
            ).astype(jnp.float32),
            lax.psum_scatter(
                part_imag.astype(jnp.bfloat16), "chan", scatter_dimension=0, tiled=True
            ).astype(jnp.float32),
        )
        mixed_real = summed_real.astype(jnp.bfloat16)
        mixed_imag = summed_imag.astype(jnp.bfloat16)
        back = back_rows(mixed_real, mixed_imag, cosine, sine)
        spectral = lax.dot_general(
            lax.all_to_all(back, "rows", split_axis=2, concat_axis=0, tiled=True),
            bwd_table,
            (((0,), (0,)), ((), ())),
            preferred_element_type=jnp.float32,
        )
        rimmed = padded_2(hidden_field, (("rows", 1),), 1)
        padded = jnp.pad(rimmed, ((0, 0), (0, 0), (1, 1)))
        local = local_conv(padded, conv_weight[layer, 0])
        summed = spectral + local + bias[layer][:, None, None]
        hidden_field = jax.nn.gelu(summed, approximate=True).astype(jnp.bfloat16)
    return hidden_field


def solution(mesh):
    in_specs = (
        P("chan", "rows", None),
        P(None, None, "chan", None, "rows", None),
        P(None, "chan", None, None, None, None),
        P(None, "chan"),
    )
    out_specs = P("chan", "rows", None)
    return jax.shard_map(body, mesh=mesh, in_specs=in_specs, out_specs=out_specs, check_vma=False)
```

profile of v0, /device:TPU:1, one launch (start us, length us, event | category | flops | bytes accessed | tf_op | source)
XLA Modules:
  0.0 340.0 jit_solution(3844635065057905590)
XLA Ops:
  0.0 2.7 copy.309
  3.5 4.4 %collective-permute-start = (bf16[16,1,4096]{2,0,1:T(8,128)(2,1)}, bf16[16,1,4096]{2,0,1:T(8,128)(2,1)S(1)}, u32[]{:S(2)}, u32[]{:S(2)}) collective-permute-start(bf16[16,1,4096]{2,0,1:T(8,128)(2,1)} %get-tuple-element.23), channel_id=1, source_target_pairs={{0,2},{2,4},{4,6},{6,8},{8,10},{10,12},{12,14},{14,16},{16,18},{18... | collective-permute-start | bytes 393224 | tf_op jit(solution)/shard_map/ppermute | solution.py:20
  9.1 8.6 %negate_convert_fusion.1 = (bf16[4096,128,1]{1,0,2:T(8,128)(2,1)S(1)}, bf16[4096,128,1]{1,0,2:T(8,128)(2,1)S(1)}) fusion(), kind=kLoop, calls=%fused_computation.114 | loop fusion | flops 8912896 | bytes 2097152 | tf_op jit(solution)/shard_map/convert.15
  19.2 6.2 %copy.291 = bf16[4096,128,2]{0,2,1:T(2,128)(2,1)} copy(bf16[4096,128,2]{1,0,2:T(8,128)(2,1)} %pad_maximum_fusion.6) | data formatting | bytes 4194304 | tf_op jit(solution)/shard_map/stack | solution.py:37
  25.5 4.2 %convert_element_type.165 = bf16[4096,256]{0,1:T(8,128)(2,1)} reshape(bf16[4096,128,2]{0,2,1:T(2,128)(2,1)} %copy.291) | data formatting | bytes 4194304 | tf_op jit(solution)/shard_map/convert_element_type | solution.py:39
  29.7 3.0 fusion.86
  35.4 12.0 %all-to-all-start = ((bf16[64,2,512]{2,1,0:T(2,128)(2,1)}), bf16[64,2,512]{2,1,0:T(2,128)(2,1)S(1)}, u32[]{:S(2)}, u32[]{:S(2)}) async-start(bf16[64,2,512]{2,1,0:T(2,128)(2,1)} %reshape.266), calls=%async_computation | async-start | bytes 262144 | tf_op jit(solution)/shard_map/all_to_all | solution.py:126
  49.0 8.6 %multiply_convert_fusion = (bf16[128,1,4096]{2,0,1:T(8,128)(2,1)S(1)}, bf16[128,1,4096]{2,0,1:T(8,128)(2,1)S(1)}) fusion(f32[128]{0:T(128)S(1)} %fusion.155), kind=kLoop, calls=%fused_computation.111 | loop fusion | flops 9961472 | bytes 2097664 | tf_op jit(solution)/shard_map/convert.6
  57.6 4.4 %fusion.154 = f32[16,16,4096]{2,0,1:T(8,128)} fusion(bf16[3,3,16,16]{3,2,1,0:T(8,128)(2,1)S(1)} %get-tuple-element.26, bf16[16,16,4096]{2,1,0:T(8,128)(2,1)S(1)} %copy-done.1), kind=kOutput, calls=%fused_computation.213 | convolution fusion | flops 33554432 | bytes 6295552 | tf_op jit(solution)/shard_map/dot_general | solution.py:102
  62.7 3.5 %copy.307 = bf16[128,2,4096]{2,1,0:T(2,128)(2,1)} copy(bf16[128,2,4096]{2,0,1:T(8,128)(2,1)S(1)} %pad_maximum_fusion.7) | data formatting | bytes 4194304 | tf_op jit(solution)/shard_map/stack | solution.py:49
  66.2 4.3 %reshape.241 = bf16[256,4096,1]{1,0,2:T(8,128)(2,1)} reshape(bf16[128,2,4096]{2,1,0:T(2,128)(2,1)} %copy.307) | data formatting | bytes 4194304 | tf_op jit(solution)/shard_map/convert_element_type | solution.py:49
  74.1 3.0 reshape.236
  81.2 2.1 fusion.102
  86.5 4.8 %all-reduce.7 = (bf16[32,2,128]{2,1,0:T(2,128)(2,1)S(1)}, bf16[32,2,128]{2,1,0:T(2,128)(2,1)S(1)}) all-reduce(bf16[32,2,128]{2,1,0:T(2,128)(2,1)S(1)} %get-tuple-element.8, bf16[32,2,128]{2,1,0:T(2,128)(2,1)S(1)} %get-tuple-element.7), channel_id=2, replica_groups=mesh['rows'=64,'chan'=2] {'chan'}, use_global_device_ids=true, to_apply=%region_1.2.clone | all-reduce | flops 16384 | bytes 65536
  95.4 2.2 fusion.98
  97.6 2.2 fusion.99
  102.4 10.2 %all-to-all-start.1 = ((bf16[64,2,512]{2,1,0:T(2,128)(2,1)}), bf16[64,2,512]{2,1,0:T(2,128)(2,1)S(1)}, u32[]{:S(2)}, u32[]{:S(2)}) async-start(bf16[64,2,512]{2,1,0:T(2,128)(2,1)} %reshape.268), calls=%async_computation.1 | async-start | bytes 262144 | tf_op jit(solution)/shard_map/all_to_all | solution.py:141
  114.1 2.6 fusion.40
  116.7 2.7 fusion.42
  119.4 2.7 fusion.44
  122.1 2.8 fusion.46
  124.8 2.7 fusion.50
  127.6 2.7 fusion.36
  130.3 2.6 fusion.48
  132.9 2.7 fusion.38
  137.0 44.9 %fusion.11 = bf16[16,16,4096]{2,1,0:T(8,128)(2,1)S(1)} fusion(bf16[256,4096,1]{1,0,2:T(8,128)(2,1)} %reshape.241, f32[16,4096,16]{1,2,0:T(8,128)} %fusion.36, f32[16,4096,16]{1,2,0:T(8,128)} %fusion.38, f32[16,4096,16]{1,2,0:T(8,128)} %fusion.40, f32[16,4096,16]{1,2,0:T(8,128)} %fusion.42, f32[16,16,4096]{2,0,1:T(8,128)} %fusion.154, ...), kind=kOutput, calls=%fused_computation.19 | convolution fusion | flops 556793856 | bytes 42074176 | tf_op jit(solution)/shard_map/dot_general | solution.py:140
  184.2 2.9 collective-permute-start.2
  191.2 10.8 %all-to-all-start.2 = ((bf16[64,2,512]{2,1,0:T(2,128)(2,1)}), bf16[64,2,512]{2,1,0:T(2,128)(2,1)S(1)}, u32[]{:S(2)}, u32[]{:S(2)}) async-start(bf16[64,2,512]{2,1,0:T(2,128)(2,1)} %reshape.270), calls=%async_computation.2 | async-start | bytes 262144 | tf_op jit(solution)/shard_map/all_to_all | solution.py:126
  202.1 5.1 %fusion.64 = f32[16,4096,16]{1,2,0:T(8,128)} fusion(bf16[16,16,4096]{2,1,0:T(8,128)(2,1)S(1)} %fusion.11, bf16[3,3,16,16]{3,2,1,0:T(8,128)(2,1)} %get-tuple-element.25), kind=kOutput, calls=%fused_computation.100 | convolution fusion | flops 33554432 | bytes 6295552 | tf_op jit(solution)/shard_map/dot_general | solution.py:102
  207.1 3.7 %all-to-all-done.2 = bf16[64,2,512]{2,1,0:T(2,128)(2,1)S(1)} async-done(((bf16[64,2,512]{2,1,0:T(2,128)(2,1)}), bf16[64,2,512]{2,1,0:T(2,128)(2,1)S(1)}, u32[]{:S(2)}, u32[]{:S(2)}) %all-to-all-start.2) | async-done | bytes 131104 | tf_op jit(solution)/shard_map/all_to_all | solution.py:126
  213.2 3.0 reshape.237
  222.3 2.2 fusion.101
  225.3 6.0 %all-reduce.6 = (bf16[32,2,128]{2,1,0:T(2,128)(2,1)S(1)}, bf16[32,2,128]{2,1,0:T(2,128)(2,1)S(1)}) all-reduce(bf16[32,2,128]{2,1,0:T(2,128)(2,1)S(1)} %get-tuple-element.6, bf16[32,2,128]{2,1,0:T(2,128)(2,1)S(1)} %get-tuple-element.5), channel_id=4, replica_groups=mesh['rows'=64,'chan'=2] {'chan'}, use_global_device_ids=true, to_apply=%region_5.6.clone | all-reduce | flops 16384 | bytes 65536
  235.5 2.2 fusion.96
  237.7 2.2 fusion.97
  242.4 5.6 %all-to-all-start.3 = ((bf16[64,2,512]{2,1,0:T(2,128)(2,1)}), bf16[64,2,512]{2,1,0:T(2,128)(2,1)S(1)}, u32[]{:S(2)}, u32[]{:S(2)}) async-start(bf16[64,2,512]{2,1,0:T(2,128)(2,1)} %reshape.272), calls=%async_computation.3 | async-start | bytes 262144 | tf_op jit(solution)/shard_map/all_to_all | solution.py:141
  248.1 2.5 pad_maximum_fusion.1
  250.6 4.4 %fusion.70 = f32[16,4096,16]{1,2,0:T(8,128)} fusion(bf16[16,16,4096]{2,1,0:T(8,128)(2,1)S(1)} %get-tuple-element.19, bf16[3,3,16,16]{3,2,1,0:T(8,128)(2,1)S(1)} %copy-done.5), kind=kOutput, calls=%fused_computation.106 | convolution fusion | flops 33554432 | bytes 6295552 | tf_op jit(solution)/shard_map/dot_general | solution.py:102
  255.0 4.4 %fusion.58 = f32[16,4096,16]{1,2,0:T(8,128)} fusion(bf16[16,16,4096]{2,1,0:T(8,128)(2,1)S(1)} %get-tuple-element.20, bf16[3,3,16,16]{3,2,1,0:T(8,128)(2,1)S(1)} %copy-done.5), kind=kOutput, calls=%fused_computation.94 | convolution fusion | flops 33554432 | bytes 6295552 | tf_op jit(solution)/shard_map/dot_general | solution.py:102
  259.4 4.3 %fusion.24 = bf16[16,18,4098]{2,1,0:T(8,128)(2,1)S(1)} fusion(bf16[16,1,4096]{2,1,0:T(2,128)(2,1)} %collective-permute-done.3, bf16[16,16,4096]{2,1,0:T(8,128)(2,1)S(1)} %fusion.11, bf16[16,1,4096]{2,1,0:T(2,128)(2,1)S(1)} %collective-permute-done.2), kind=kLoop, calls=%fused_computation.48 | loop fusion | flops 14162688 | bytes 4719744 | tf_op jit(solution)/shard_map/concatenate | solution.py:24
  263.8 4.3 %fusion.223 = (bf16[16,16,4096]{2,1,0:T(8,128)(2,1)S(1)}, bf16[16,16,4096]{2,1,0:T(8,128)(2,1)S(1)}, bf16[16,16,4096]{2,1,0:T(8,128)(2,1)S(1)}, bf16[16,16,4096]...) fusion(bf16[16,18,4098]{2,1,0:T(8,128)(2,1)S(1)} %fusion.24), kind=kLoop, calls=%fused_computation.294 | loop fusion | bytes 25165824 | tf_op jit(solution)/shard_map/slice | solution.py:101
  268.1 4.5 %fusion.72 = f32[16,4096,16]{1,2,0:T(8,128)} fusion(bf16[16,16,4096]{2,1,0:T(8,128)(2,1)S(1)} %get-tuple-element.13, bf16[3,3,16,16]{3,2,1,0:T(8,128)(2,1)S(1)} %copy-done.5), kind=kOutput, calls=%fused_computation.108 | convolution fusion | flops 33554432 | bytes 6295552 | tf_op jit(solution)/shard_map/dot_general | solution.py:102
  272.5 4.4 %fusion.60 = f32[16,4096,16]{1,2,0:T(8,128)} fusion(bf16[16,16,4096]{2,1,0:T(8,128)(2,1)S(1)} %get-tuple-element.14, bf16[3,3,16,16]{3,2,1,0:T(8,128)(2,1)S(1)} %copy-done.5), kind=kOutput, calls=%fused_computation.96 | convolution fusion | flops 33554432 | bytes 6295552 | tf_op jit(solution)/shard_map/dot_general | solution.py:102
  276.9 4.4 %fusion.62 = f32[16,4096,16]{1,2,0:T(8,128)} fusion(bf16[16,16,4096]{2,1,0:T(8,128)(2,1)S(1)} %get-tuple-element.15, bf16[3,3,16,16]{3,2,1,0:T(8,128)(2,1)S(1)} %copy-done.5), kind=kOutput, calls=%fused_computation.98 | convolution fusion | flops 33554432 | bytes 6295552 | tf_op jit(solution)/shard_map/dot_general | solution.py:102
  281.3 4.4 %fusion.66 = f32[16,4096,16]{1,2,0:T(8,128)} fusion(bf16[16,16,4096]{2,1,0:T(8,128)(2,1)S(1)} %get-tuple-element.16, bf16[3,3,16,16]{3,2,1,0:T(8,128)(2,1)S(1)} %copy-done.5), kind=kOutput, calls=%fused_computation.102 | convolution fusion | flops 33554432 | bytes 6295552 | tf_op jit(solution)/shard_map/dot_general | solution.py:102
  285.7 4.4 %fusion.68 = f32[16,4096,16]{1,2,0:T(8,128)} fusion(bf16[16,16,4096]{2,1,0:T(8,128)(2,1)S(1)} %get-tuple-element.17, bf16[3,3,16,16]{3,2,1,0:T(8,128)(2,1)S(1)} %copy-done.5), kind=kOutput, calls=%fused_computation.104 | convolution fusion | flops 33554432 | bytes 6295552 | tf_op jit(solution)/shard_map/dot_general | solution.py:102
  290.1 4.3 %fusion.56 = f32[16,4096,16]{1,2,0:T(8,128)} fusion(bf16[16,16,4096]{2,1,0:T(8,128)(2,1)S(1)} %get-tuple-element.18, bf16[3,3,16,16]{3,2,1,0:T(8,128)(2,1)S(1)} %copy-done.5), kind=kOutput, calls=%fused_computation.92 | convolution fusion | flops 33554432 | bytes 6295552 | tf_op jit(solution)/shard_map/dot_general | solution.py:102
  297.7 41.9 %fusion.19 = bf16[16,16,4096]{2,1,0:T(8,128)(2,1)} fusion(bf16[256,4096,1]{1,0,2:T(8,128)(2,1)S(1)} %copy-done, f32[16,4096,16]{1,2,0:T(8,128)} %fusion.56, f32[16,4096,16]{1,2,0:T(8,128)} %fusion.58, f32[16,4096,16]{1,2,0:T(8,128)} %fusion.60, f32[16,4096,16]{1,2,0:T(8,128)} %fusion.62, f32[16,4096,16]{1,2,0:T(8,128)} %fusion.64, ...), kind=kOutput, calls=%fused_computation.27 | convolution fusion | flops 556793856 | bytes 42074176 | tf_op jit(solution)/shard_map/dot_general | solution.py:140
  (80 shorter events, 53.9 us)
Async XLA Ops:
  3.5 109.1 %collective-permute-start = (bf16[16,1,4096]{2,0,1:T(8,128)(2,1)}, bf16[16,1,4096]{2,0,1:T(8,128)(2,1)S(1)}, u32[]{:S(2)}, u32[]{:S(2)}) collective-permute-start(bf16[16,1,4096]{2,0,1:T(8,128)(2,1)} %get-tuple-element.23), channel_id=1, source_target_pairs={{0,2},{2,4},{4,6},{6,8},{8,10},{10,12},{12,14},{14,16},{16,18},{18... | collective-permute-start | bytes 393224 | tf_op jit(solution)/shard_map/ppermute | solution.py:20
  7.8 104.8 %collective-permute-start.1 = (bf16[16,1,4096]{2,0,1:T(8,128)(2,1)}, bf16[16,1,4096]{2,0,1:T(8,128)(2,1)S(1)}, u32[]{:S(2)}, u32[]{:S(2)}) collective-permute-start(bf16[16,1,4096]{2,0,1:T(8,128)(2,1)} %get-tuple-element.24), channel_id=1, source_target_pairs={{2,0},{4,2},{6,4},{8,6},{10,8},{12,10},{14,12},{16,14},{18,16},{20... | collective-permute-start | bytes 393224 | tf_op jit(solution)/shard_map/ppermute | solution.py:23
  35.4 36.4 %all-to-all-start = ((bf16[64,2,512]{2,1,0:T(2,128)(2,1)}), bf16[64,2,512]{2,1,0:T(2,128)(2,1)S(1)}, u32[]{:S(2)}, u32[]{:S(2)}) async-start(bf16[64,2,512]{2,1,0:T(2,128)(2,1)} %reshape.266), calls=%async_computation | async-start | bytes 262144 | tf_op jit(solution)/shard_map/all_to_all | solution.py:126
  47.4 10.2 %copy-start.1 = (bf16[16,16,4096]{2,1,0:T(8,128)(2,1)S(1)}, bf16[16,16,4096]{2,1,0:T(8,128)(2,1)}, u32[]{:S(2)}) copy-start(bf16[16,16,4096]{2,1,0:T(8,128)(2,1)} %param.4) | copy-start | bytes 6291460
  49.0 13.0 %copy-start.6 = (bf16[3,3,16,16]{3,2,1,0:T(8,128)(2,1)}, bf16[3,3,16,16]{3,2,1,0:T(8,128)(2,1)S(1)}, u32[]{:S(2)}) copy-start(bf16[3,3,16,16]{3,2,1,0:T(8,128)(2,1)S(1)} %get-tuple-element.26) | copy-start | bytes 13828
  62.0 0.7 copy-start.8
  66.2 4.3 %copy-start.9 = (u32[128]{0:T(128)S(1)}, u32[128]{0:T(128)}, u32[]{:S(2)}) copy-start(u32[128]{0:T(128)} %constant.73) | copy-start | bytes 1540
  81.2 4.2 %copy-start.2 = (f32[2,2,16,32,2,128]{5,4,3,2,1,0:T(2,128)S(1)}, f32[2,2,16,32,2,128]{5,4,3,2,1,0:T(2,128)}, u32[]{:S(2)}) copy-start(f32[2,2,16,32,2,128]{5,4,3,2,1,0:T(2,128)} %param.5) | copy-start | bytes 6291460
  102.4 33.2 %all-to-all-start.1 = ((bf16[64,2,512]{2,1,0:T(2,128)(2,1)}), bf16[64,2,512]{2,1,0:T(2,128)(2,1)S(1)}, u32[]{:S(2)}, u32[]{:S(2)}) async-start(bf16[64,2,512]{2,1,0:T(2,128)(2,1)} %reshape.268), calls=%async_computation.1 | async-start | bytes 262144 | tf_op jit(solution)/shard_map/all_to_all | solution.py:141
  112.6 1.5 copy-start.7
  137.0 44.9 %copy-start.4 = (bf16[4096,256]{0,1:T(8,128)(2,1)S(1)}, bf16[4096,256]{0,1:T(8,128)(2,1)}, u32[]{:S(2)}) copy-start(bf16[4096,256]{0,1:T(8,128)(2,1)} %convert_element_type.165) | copy-start | bytes 6291460
  184.2 63.9 %collective-permute-start.2 = (bf16[16,1,4096]{2,1,0:T(2,128)(2,1)}, bf16[16,1,4096]{2,1,0:T(2,128)(2,1)S(1)}, u32[]{:S(2)}, u32[]{:S(2)}) collective-permute-start(bf16[16,1,4096]{2,1,0:T(2,128)(2,1)} %get-tuple-element.21), channel_id=1, source_target_pairs={{0,2},{2,4},{4,6},{6,8},{8,10},{10,12},{12,14},{14,16},{16,18},{18... | collective-permute-start | bytes 393224 | tf_op jit(solution)/shard_map/ppermute | solution.py:20
  187.2 60.9 %collective-permute-start.3 = (bf16[16,1,4096]{2,1,0:T(2,128)(2,1)}, bf16[16,1,4096]{2,1,0:T(2,128)(2,1)}, u32[]{:S(2)}, u32[]{:S(2)}) collective-permute-start(bf16[16,1,4096]{2,1,0:T(2,128)(2,1)} %get-tuple-element.22), channel_id=1, source_target_pairs={{2,0},{4,2},{6,4},{8,6},{10,8},{12,10},{14,12},{16,14},{18,16},{20... | collective-permute-start | bytes 393224 | tf_op jit(solution)/shard_map/ppermute | solution.py:23
  191.2 19.6 %all-to-all-start.2 = ((bf16[64,2,512]{2,1,0:T(2,128)(2,1)}), bf16[64,2,512]{2,1,0:T(2,128)(2,1)S(1)}, u32[]{:S(2)}, u32[]{:S(2)}) async-start(bf16[64,2,512]{2,1,0:T(2,128)(2,1)} %reshape.270), calls=%async_computation.2 | async-start | bytes 262144 | tf_op jit(solution)/shard_map/all_to_all | solution.py:126
  220.2 4.4 %copy-start.3 = (f32[2,2,16,32,2,128]{5,4,3,2,1,0:T(2,128)S(1)}, f32[2,2,16,32,2,128]{5,4,3,2,1,0:T(2,128)}, u32[]{:S(2)}) copy-start(f32[2,2,16,32,2,128]{5,4,3,2,1,0:T(2,128)} %param.5) | copy-start | bytes 6291460
  242.4 52.0 %all-to-all-start.3 = ((bf16[64,2,512]{2,1,0:T(2,128)(2,1)}), bf16[64,2,512]{2,1,0:T(2,128)(2,1)S(1)}, u32[]{:S(2)}, u32[]{:S(2)}) async-start(bf16[64,2,512]{2,1,0:T(2,128)(2,1)} %reshape.272), calls=%async_computation.3 | async-start | bytes 262144 | tf_op jit(solution)/shard_map/all_to_all | solution.py:141
  248.1 2.5 copy-start.5
  294.4 3.3 copy-start
where the time goes:
time: 346 us; the launch traced here: 340 us
  matrix products  191 us (55%)
  local copies, waits for them, and re-layouts  55.9 us (16%)
  starting transfers between devices  48.5 us (14%)
  other arithmetic  29 us (8%)
  blocking collectives  10.7 us (3%)
  waiting for transfers between devices  3.71 us (1%)
    dot_general x2, matrix products, body(): lax.dot_general(lax.all_to_all(back, 'rows', split_axis=2, concat_axis=0,...  86.8 us
    dot_general x18, matrix products, local_conv(): lax.dot_general(taps[row_off, col_off], window, (((1,), (0,)), ((), ())),...  66.1 us
    all_to_all x2, starting transfers between devices, body(): lax.all_to_all(row_modes, 'rows', split_axis=0, concat_axis=2, tiled=True)  22.9 us
    another operation x2, other arithmetic  17.2 us
    all_to_all x2, starting transfers between devices, body(): lax.all_to_all(back, 'rows', split_axis=2, concat_axis=0, tiled=True)  15.8 us
    unnamed x34, local copies, waits for them, and re-layouts  14.9 us
    unnamed x2, blocking collectives  10.7 us
    concatenate x3, other arithmetic, padded_2(): block = jnp.concatenate([low, block, high], axis=dim)  8.29 us
  transfers between devices with their start and end apart: 8, of which 1 were waited for; matrix products, arithmetic and copies ran while one was open for 52% of the time, Pallas kernels for 0%

commit v1 on v0

v1 whole, which is shorter than its diff:
```python
import functools
import math

import jax
import jax.numpy as jnp
import ml_dtypes
import numpy as np
from jax import lax
from jax.experimental import pallas as pl
from jax.experimental.pallas import tpu as pltpu
from jax.sharding import PartitionSpec as P

M = 128
LAYERS = 2
N = 64
CG = 16
XR = 16
NY = 4096
NX = N * XR
CX = CG * XR
TILE = 512
CHUNKS = 4
F32 = jnp.float32
BF16 = jnp.bfloat16
MESH = pl.DeviceIdType.MESH


def np_angles(count, freqs, length):
    products = (np.arange(count, dtype=np.int64)[:, None] * freqs[None, :]) % length
    return products.astype(np.float32) * np.float32(2.0 * math.pi / length)


def column_table():
    angles = np_angles(NY, np.arange(M), NY)
    both = np.stack([np.cos(angles), -np.sin(angles)], axis=2).reshape(NY, 2 * M)
    return np.ascontiguousarray(both.T).astype(ml_dtypes.bfloat16)


def row_table():
    j = np.arange(M)
    freqs = np.where(j < M // 2, j, NX - M + j)
    angles = np_angles(NX, freqs, NX)
    cosine = np.cos(angles).astype(ml_dtypes.bfloat16).reshape(N, XR, M).transpose(1, 0, 2)
    sine = np.sin(angles).astype(ml_dtypes.bfloat16).reshape(N, XR, M).transpose(1, 0, 2)
    real = np.concatenate([cosine, -sine], axis=2)
    imag = np.concatenate([sine, cosine], axis=2)
    return np.stack([real, imag], axis=1).reshape(XR * 2 * N, 2 * M)


def dot(a, b):
    return lax.dot_general(a, b, (((1,), (0,)), ((), ())), preferred_element_type=F32)


def dot_nt(a, b):
    return lax.dot_general(a, b, (((1,), (1,)), ((), ())), preferred_element_type=F32)


def gelu(v):
    return 0.5 * v * (1.0 + jnp.tanh(0.7978845608 * (v + 0.044715 * (v * v * v))))


def iota(shape, dim):
    return lax.broadcasted_iota(jnp.int32, shape, dim)


def kernel(
    field,
    table,
    rtable,
    weight,
    taps,
    bias,
    out,
    h,
    ft,
    rt,
    wt,
    hm,
    hp,
    acc,
    modes,
    snd,
    rcv,
    blk,
    ysc,
    lhs,
    usc,
    vs,
    vr,
    vrow,
    spec,
    conv_main,
    conv_edge,
    e_snd,
    e_rcv,
    e3,
    ld_sem,
    a_send,
    a_recv,
    c_send,
    c_recv,
    e_send,
    e_recv,
    o_sem,
):
    me = lax.axis_index("rows")
    chan = lax.axis_index("chan")
    width = NY // CHUNKS

    loads = []
    for i in range(CHUNKS):
        cols = pl.ds(i * width, width)
        loads.append(
            (
                pltpu.make_async_copy(table.at[:, cols], ft.at[:, cols], ld_sem.at[2 * i]),
                pltpu.make_async_copy(field.at[:, cols], h.at[:, cols], ld_sem.at[2 * i + 1]),
            )
        )
    load_rt = pltpu.make_async_copy(rtable, rt, ld_sem.at[2 * CHUNKS])
    load_wt = pltpu.make_async_copy(weight, wt, ld_sem.at[2 * CHUNKS + 1])
    for one, two in loads:
        one.start()
        two.start()
    load_rt.start()
    load_wt.start()

    barrier = pltpu.get_barrier_semaphore()

    def greet(i, carry):
        pl.semaphore_signal(
            barrier, inc=1, device_id={"rows": lax.rem(me + i, N)}, device_id_type=MESH
        )
        return carry

    lax.fori_loop(1, N, greet, 0)
    pl.semaphore_signal(barrier, inc=1, device_id={"chan": 1 - chan}, device_id_type=MESH)

    def partner(i):
        y = lax.rem(me // 16 + i // 16, 4)
        x = lax.rem(me // 4 + i // 4, 4)
        z = lax.rem(me + i, 4)
        return y * 16 + x * 4 + z

    def exchange(index):
        src, dst = snd.at[index], rcv.at[index]

        def go(i, carry):
            d = partner(i)
            pltpu.make_async_remote_copy(
                src_ref=src.at[d],
                dst_ref=dst.at[me],
                send_sem=a_send.at[index],
                recv_sem=a_recv.at[index],
                device_id={"rows": d},
                device_id_type=MESH,
            ).start()
            return carry

        lax.fori_loop(1, N, go, 0)
        pltpu.make_async_copy(src.at[me], dst.at[me], a_recv.at[index]).start()

    def exchange_done(index):
        dst = rcv.at[index]
        pltpu.make_async_copy(dst, dst, a_recv.at[index]).wait()

    def edge_copies(layer):
        up = lax.rem(me + 1, N)
        down = lax.rem(me + N - 1, N)
        return [
            pltpu.make_async_remote_copy(
                src_ref=e_snd.at[layer, side],
                dst_ref=e_rcv.at[layer, side],
                send_sem=e_send.at[layer, side],
                recv_sem=e_recv.at[layer, side],
                device_id={"rows": to},
                device_id_type=MESH,
            )
            for side, to in ((0, up), (1, down))
        ]

    def pack_rows():
        shaped = modes[...].reshape(N // 2, 8, CX)
        a, b = shaped[:, :, :128], shaped[:, :, 128:]
        low = iota((N // 2, 8, 128), 1) < 4
        even = jnp.where(low, a, pltpu.roll(b, 4, 1))
        odd = jnp.where(low, pltpu.roll(a, 4, 1), b)
        return even.astype(BF16), odd.astype(BF16)

    def conv_matrices(layer):
        row = iota((CX, CX), 0) & (XR - 1)
        col = iota((CX, CX), 1) & (XR - 1)
        out_of = ((iota((CX, CG), 0) >> 4) == iota((CX, CG), 1)).astype(F32).astype(BF16)
        in_of = ((iota((CG, CX), 1) >> 4) == iota((CG, CX), 0)).astype(F32).astype(BF16)
        xr = iota((CX, CG), 0) & (XR - 1)
        edge = jnp.zeros((CX, 128), F32)
        for s in range(3):
            total = jnp.zeros((CX, CX), F32)
            for r in range(3):
                tap = dot(out_of, taps[layer, r, s])
                total = jnp.where(col == row + (r - 1), dot(tap.astype(BF16), in_of), total)
                if r != 1:
                    side = 0 if r == 0 else 1
                    at = 0 if r == 0 else XR - 1
                    outer = (me == 0) if r == 0 else (me == N - 1)
                    keep = jnp.where(outer, -1, at)
                    offset = s * 32 + side * CG
                    place = (iota((CG, 128), 1) == iota((CG, 128), 0) + offset).astype(F32)
                    part = jnp.where(xr == keep, tap, 0.0).astype(BF16)
                    edge = edge + dot(part, place.astype(BF16))
            conv_main[layer, s] = total.astype(BF16)
        conv_edge[layer] = edge.astype(BF16)

    def edges_out(layer):
        side = iota((32, CX), 0) >> 4
        want = (iota((32, CX), 0) & 15) * XR + jnp.where(side == 0, XR - 1, 0)
        pick = (iota((32, CX), 1) == want).astype(F32).astype(BF16)

        def step(t, carry):
            cols = pl.ds(pl.multiple_of(t * TILE, TILE), TILE)
            rows = dot(pick, h[:, cols]).astype(BF16)
            e_snd[layer, 0, :, cols] = rows[:CG]
            e_snd[layer, 1, :, cols] = rows[CG:]
            return carry

        lax.fori_loop(0, NY // TILE, step, 0)
        for copy in edge_copies(layer):
            copy.start()

    def shifted(block):
        wide = block.astype(F32)
        lane = iota(wide.shape, 1)
        before = jnp.where(lane == 0, 0.0, pltpu.roll(wide, 1, 1))
        after = jnp.where(lane == NY - 1, 0.0, pltpu.roll(wide, NY - 1, 1))
        return before.astype(BF16), after.astype(BF16)

    def shift_field():
        def step(i, carry):
            rows = pl.ds(pl.multiple_of(i * 16, 16), 16)
            before, after = shifted(h[rows, :])
            hm[rows, :] = before
            hp[rows, :] = after
            return carry

        lax.fori_loop(0, CX // 16, step, 0)

    def convolve(layer):
        for copy in edge_copies(layer):
            copy.wait()
        for side in range(2):
            block = e_rcv[layer, side]
            before, after = shifted(block)
            e3[pl.ds(side * CG, CG), :] = before
            e3[pl.ds(32 + side * CG, CG), :] = block
            e3[pl.ds(64 + side * CG, CG), :] = after
        e3[pl.ds(96, 32), :] = jnp.zeros((32, NY), BF16)

        def step(t, carry):
            cols = pl.ds(pl.multiple_of(t * TILE, TILE), TILE)
            total = dot(conv_main[layer, 0], hm[:, cols])
            total += dot(conv_main[layer, 1], h[:, cols])
            total += dot(conv_main[layer, 2], hp[:, cols])
            total += dot(conv_edge[layer], e3[:, cols])
            acc[:, cols] = total + bias[layer]
            return carry

        lax.fori_loop(0, NY // TILE, step, 0)

    def mix(layer):
        blk[...] = rcv[2 * layer].astype(F32).reshape(N * 8, 128)
        for kk in range(2):
            for half in range(2):
                parts = [blk[pl.ds(half * 4 + 2 * kk + p, N, stride=8), :] for p in range(2)]
                ysc[2 * kk + half] = jnp.concatenate(parts, axis=0).T
        for x in range(XR):
            rows = [ysc[i, pl.ds(x, 8, stride=XR), :] for i in range(4)]
            lhs[:, pl.ds(x * 128, 128)] = jnp.concatenate(rows, axis=0).astype(BF16)
        usc[...] = dot(lhs[...], rt[...])
        odd = (iota((8, 128), 0) & 1) == 1
        real = jnp.zeros((8, 8, 128), F32)
        imag = jnp.zeros((8, 8, 128), F32)
        for c in range(CG):
            ur, ui = [
                jnp.where(
                    odd,
                    jnp.broadcast_to(usc[pl.ds(CG + c, 1), pl.ds(p * 128, 128)], (8, 128)),
                    jnp.broadcast_to(usc[pl.ds(c, 1), pl.ds(p * 128, 128)], (8, 128)),
                )[None]
                for p in range(2)
            ]
            wr = wt[layer, 0, c].reshape(8, 8, 128)
            wi = wt[layer, 1, c].reshape(8, 8, 128)
            real += wr * ur - wi * ui
            imag += wr * ui + wi * ur
        vs[layer, :, 0] = real.reshape(2, 32, 128)
        vs[layer, :, 1] = imag.reshape(2, 32, 128)

    def mixed_copy(layer):
        return pltpu.make_async_remote_copy(
            src_ref=vs.at[layer, 1 - chan],
            dst_ref=vr.at[layer],
            send_sem=c_send.at[layer],
            recv_sem=c_recv.at[layer],
            device_id={"chan": 1 - chan},
            device_id_type=MESH,
        )

    def back_rows(layer):
        vrow[...] = vs[layer, chan] + vr[layer]
        mixed = jnp.concatenate(
            [
                jnp.concatenate([vrow[p, pl.ds(kk, CG, stride=2), :] for kk in range(2)], axis=0)
                for p in range(2)
            ],
            axis=1,
        ).astype(BF16)
        for x in range(XR):
            piece = dot_nt(mixed, rt[pl.ds(x * 128, 128), :])
            for i in range(4):
                ysc[i, pl.ds(x, 8, stride=XR), :] = piece[8 * i : 8 * i + 8]
        scale = 2.0 / (M * math.sqrt(NX * NY))
        for kk in range(2):
            first = jnp.where(me == 0, 0.5 * scale, scale) if kk == 0 else scale
            for half in range(2):
                flipped = ysc[2 * kk + half].T * first
                for p in range(2):
                    blk[pl.ds(half * 4 + 2 * kk + p, N, stride=8), :] = flipped[
                        p * N : p * N + N
                    ]
        snd[2 * layer + 1] = blk[...].reshape(N, 8, 128).astype(BF16)

    def spectral_rows(layer):
        wide = rcv[2 * layer + 1].astype(F32).reshape(N // 2, 2, 8, 128)
        even, odd = wide[:, 0], wide[:, 1]
        low = iota((N // 2, 8, 128), 1) < 4
        a = jnp.where(low, even, pltpu.roll(odd, 4, 1)).reshape(CX, 128)
        b = jnp.where(low, pltpu.roll(even, 4, 1), odd).reshape(CX, 128)
        spec[pl.ds(0, 128), :] = a.T.astype(BF16)
        spec[pl.ds(128, 128), :] = b.T.astype(BF16)

    def forward_send(layer):
        even, odd = pack_rows()
        view = snd.at[2 * layer]
        for i in range(N // 2):
            view[2 * i] = even[i]
            view[2 * i + 1] = odd[i]

    modes[...] = jnp.zeros_like(modes)
    for i in range(CHUNKS):
        cols = pl.ds(i * width, width)
        loads[i][0].wait()
        loads[i][1].wait()
        modes[...] += dot_nt(ft[:, cols], h[:, cols])

    for layer in range(LAYERS):
        forward_send(layer)
        if layer == 0:
            pl.semaphore_wait(barrier, N)
        exchange(2 * layer)
        edges_out(layer)
        if layer == 0:
            for each in range(LAYERS):
                conv_matrices(each)
            load_rt.wait()
            load_wt.wait()
        shift_field()
        exchange_done(2 * layer)
        mix(layer)
        mixed_copy(layer).start()
        mixed_copy(layer).wait()
        back_rows(layer)
        exchange(2 * layer + 1)
        convolve(layer)
        exchange_done(2 * layer + 1)
        spectral_rows(layer)
        last = layer == LAYERS - 1
        if not last:
            modes[...] = jnp.zeros_like(modes)

        def step(t, carry):
            cols = pl.ds(pl.multiple_of(t * TILE, TILE), TILE)
            value = gelu(acc[:, cols] + dot(spec[...], ft[:, cols])).astype(BF16)
            h[:, cols] = value
            if last:
                pltpu.make_async_copy(h.at[:, cols], out.at[:, cols], o_sem.at[t]).start()
            else:
                modes[...] += dot_nt(ft[:, cols], value)
            return carry

        lax.fori_loop(0, NY // TILE, step, 0)

    def drain(t, carry):
        cols = pl.ds(pl.multiple_of(t * TILE, TILE), TILE)
        pltpu.make_async_copy(h.at[:, cols], out.at[:, cols], o_sem.at[t]).wait()
        return carry

    lax.fori_loop(0, NY // TILE, drain, 0)
    for index in range(2 * LAYERS):
        sent = snd.at[index, pl.ds(0, N - 1)]
        pltpu.make_async_copy(sent, sent, a_send.at[index]).wait()


def body(field, spec_weight, conv_weight, bias):
    flat = field.reshape(CX, NY)
    weight = spec_weight.reshape(LAYERS, 2, CG, 64, 128)
    taps = conv_weight.reshape(LAYERS, 3, 3, CG, CG)
    wide_bias = jnp.broadcast_to(bias[:, :, None, None], (LAYERS, CG, XR, 1)).reshape(LAYERS, CX, 1)
    anywhere = pl.BlockSpec(memory_space=pl.ANY)
    vmem = pl.BlockSpec(memory_space=pltpu.VMEM)
    result = pl.pallas_call(
        kernel,
        out_shape=jax.ShapeDtypeStruct((CX, NY), BF16),
        in_specs=[anywhere, anywhere, anywhere, anywhere, vmem, vmem],
        out_specs=anywhere,
        scratch_shapes=[
            pltpu.VMEM((CX, NY), BF16),
            pltpu.VMEM((2 * M, NY), BF16),
            pltpu.VMEM((XR * 2 * N, 2 * M), BF16),
            pltpu.VMEM((LAYERS, 2, CG, 64, 128), F32),
            pltpu.VMEM((CX, NY), BF16),
            pltpu.VMEM((CX, NY), BF16),
            pltpu.VMEM((CX, NY), F32),
            pltpu.VMEM((2 * M, CX), F32),
            pltpu.VMEM((2 * LAYERS, N, 8, 128), BF16),
            pltpu.VMEM((2 * LAYERS, N, 8, 128), BF16),
            pltpu.VMEM((N * 8, 128), F32),
            pltpu.VMEM((4, 128, 128), F32),
            pltpu.VMEM((32, XR * 128), BF16),
            pltpu.VMEM((32, 256), F32),
            pltpu.VMEM((LAYERS, 2, 2, 32, 128), F32),
            pltpu.VMEM((LAYERS, 2, 32, 128), F32),
            pltpu.VMEM((2, 32, 128), F32),
            pltpu.VMEM((CX, 2 * M), BF16),
            pltpu.VMEM((LAYERS, 3, CX, CX), BF16),
            pltpu.VMEM((LAYERS, CX, 128), BF16),
            pltpu.VMEM((LAYERS, 2, CG, NY), BF16),
            pltpu.VMEM((LAYERS, 2, CG, NY), BF16),
            pltpu.VMEM((128, NY), BF16),
            pltpu.SemaphoreType.DMA((2 * CHUNKS + 2,)),
            pltpu.SemaphoreType.DMA((2 * LAYERS,)),
            pltpu.SemaphoreType.DMA((2 * LAYERS,)),
            pltpu.SemaphoreType.DMA((LAYERS,)),
            pltpu.SemaphoreType.DMA((LAYERS,)),
            pltpu.SemaphoreType.DMA((LAYERS, 2)),
            pltpu.SemaphoreType.DMA((LAYERS, 2)),
            pltpu.SemaphoreType.DMA((NY // TILE,)),
        ],
        compiler_params=pltpu.CompilerParams(
            collective_id=0, has_side_effects=True, vmem_limit_bytes=56 * 2**20
        ),
        cost_estimate=pl.CostEstimate(
            flops=6 * 10**9, bytes_accessed=10 * 2**20, transcendentals=2 * CX * NY
        ),
        name="fourier_layers",
    )(flat, jnp.asarray(column_table()), jnp.asarray(row_table()), weight, taps, wide_bias)
    return result.reshape(CG, XR, NY)


def solution(mesh):
    in_specs = (
        P("chan", "rows", None),
        P(None, None, "chan", None, "rows", None),
        P(None, "chan", None, None, None, None),
        P(None, "chan"),
    )
    out_specs = P("chan", "rows", None)
    return jax.shard_map(body, mesh=mesh, in_specs=in_specs, out_specs=out_specs, check_vma=False)
```

time: 346 us -> 56.6 us (0.16); the launches traced: 340 us -> 56.4 us
  matrix products: 191 us -> 0 us
  Pallas kernels: 0 us -> 51.6 us
  local copies, waits for them, and re-layouts: 55.9 us -> 4.75 us
  starting transfers between devices: 48.5 us -> 0 us
  other arithmetic: 29 us -> 0 us
  blocking collectives: 10.7 us -> 0 us
  waiting for transfers between devices: 3.71 us -> 0 us
    dot_general x38 -> x0, matrix products: 191 us -> none  [the longest x2 86.8 us: body(): lax.dot_general(lax.all_to_all(back, 'rows', split_axis=2, concat_axis=0,...]
    pallas_call x0 -> x1, Pallas kernels: none -> 51.6 us  [body(): pl.pallas_call(kernel, out_shape=jax.ShapeDtypeStruct((CX, NY), BF16), in...]
    all_to_all x4 -> x0, starting transfers between devices: 38.7 us -> none  [the longest x2 22.9 us: body(): lax.all_to_all(row_modes, 'rows', split_axis=0, concat_axis=2, tiled=True)]
    another operation x6 -> x0, other arithmetic: 18.9 us -> none
    unnamed x34 -> x1, local copies, waits for them, and re-layouts: 14.9 us -> 3.13 us
    convert_element_type x6 -> x0, local copies, waits for them, and re-layouts: 11.7 us -> none  [the longest x1 4.26 us: backward_table(): jnp.stack([cosine, -sine], axis=1).reshape(2 * modes, columns)]
    unnamed x2 -> x0, blocking collectives: 10.7 us -> none
    ppermute x4 -> x0, starting transfers between devices: 9.87 us -> none  [the longest x2 7.28 us: padded_2(): lax.ppermute(lax.slice_in_dim(block, block.shape[dim] - width, None, axis...]
  transfers between devices with their start and end apart: 8 -> 0, of which waited for: 1 -> 0; matrix products, arithmetic and copies ran while one was open for 52% -> 0% of each run, Pallas kernels for 0% -> 0%
where the time goes in v1:
time: 56.6 us; the launch traced here: 56.4 us
  Pallas kernels  51.6 us (91%)
  local copies, waits for them, and re-layouts  4.75 us (8%)
    pallas_call x1, Pallas kernels, body(): pl.pallas_call(kernel, out_shape=jax.ShapeDtypeStruct((CX, NY), BF16), in...  51.6 us
    unnamed x1, local copies, waits for them, and re-layouts  3.13 us
    broadcast_in_dim x2, local copies, waits for them, and re-layouts, body(): jnp.broadcast_to(bias[:, :, None, None], (LAYERS, CG, XR, 1))  1.62 us

profile of v1, /device:TPU:1, one launch (start us, length us, event | category | flops | bytes accessed | tf_op | source)
XLA Modules:
  0.0 56.4 jit_solution(12933781210709200148)
XLA Ops:
  0.0 0.7 %broadcast_in_dim.8 = f32[2,16,16]{2,1,0:T(8,128)S(1)} broadcast(f32[2,16]{1,0:T(2,128)} %param.9), dimensions={0,1} | broadcast | bytes 2176 | tf_op jit(solution)/shard_map/broadcast_in_dim | solution.py:406
  0.7 0.9 %broadcast_in_dim.10.bias = f32[2,256,1]{2,1,0:T(8,128)} reshape(f32[2,16,16]{2,1,0:T(8,128)S(1)} %broadcast_in_dim.8) | data formatting | bytes 4096 | tf_op jit(solution)/shard_map/broadcast_in_dim | solution.py:406
  1.6 51.6 %fourier_layers.1 = bf16[256,4096]{1,0:T(8,128)(2,1)} custom-call(bf16[256,4096]{1,0:T(8,128)(2,1)} %bitcast.5, bf16[256,4096]{1,0:T(8,128)(2,1)} %constant.4.clone.table, bf16[2048,256]{1,0:T(8,128)(2,1)} %constant.5.clone.rtable, f32[2,2,16,64,128]{4,3,2,1,0:T(8,128)} %bitcast.6, bf16[2,3,3,16,16]{4,3,2,1,0:T(8,128)(2,1)} %bitcast.7, ...), custom_call_target="tpu_custom_call" | custom-call | flops 6000000000 | bytes 10485760 | tf_op jit(solution)/shard_map/fourier_layers/pallas_call | solution.py:409
  53.3 3.1 %copy.9 = bf16[16,16,4096]{2,1,0:T(8,128)(2,1)} copy(bf16[16,16,4096]{2,1,0:T(8,128)(2,1)} %bitcast.4) | data formatting | bytes 4194304

commit v2 on v1

--- a/solution.py
+++ b/solution.py
@@ -18,11 +18,22 @@
 NY = 4096
 NX = N * XR
 CX = CG * XR
-TILE = 512
+TILE = 1024
+TILES = NY // TILE
 CHUNKS = 4
 F32 = jnp.float32
 BF16 = jnp.bfloat16
 MESH = pl.DeviceIdType.MESH
+
+
+def hops(offset):
+    return sum(min(d, 4 - d) for d in offset)
+
+
+OFFSETS = sorted(
+    [(y, x, z) for y in range(4) for x in range(4) for z in range(4)][1:],
+    key=lambda offset: -hops(offset),
+)
 
 
 def np_angles(count, freqs, length):
@@ -68,13 +79,16 @@
     table,
     rtable,
     weight,
-    taps,
-    bias,
+    taps_any,
+    bias_any,
     out,
     h,
     ft,
     rt,
     wt,
+    taps,
+    bias,
+    bias_col,
     hm,
     hp,
     acc,
@@ -118,9 +132,13 @@
         )
     load_rt = pltpu.make_async_copy(rtable, rt, ld_sem.at[2 * CHUNKS])
     load_wt = pltpu.make_async_copy(weight, wt, ld_sem.at[2 * CHUNKS + 1])
+    load_taps = pltpu.make_async_copy(taps_any, taps, ld_sem.at[2 * CHUNKS + 2])
+    load_bias = pltpu.make_async_copy(bias_any, bias, ld_sem.at[2 * CHUNKS + 3])
     for one, two in loads:
         one.start()
         two.start()
+    load_taps.start()
+    load_bias.start()
     load_rt.start()
     load_wt.start()
 
@@ -135,17 +153,14 @@
     lax.fori_loop(1, N, greet, 0)
     pl.semaphore_signal(barrier, inc=1, device_id={"chan": 1 - chan}, device_id_type=MESH)
 
-    def partner(i):
-        y = lax.rem(me // 16 + i // 16, 4)
-        x = lax.rem(me // 4 + i // 4, 4)
-        z = lax.rem(me + i, 4)
-        return y * 16 + x * 4 + z
+    ys = [lax.rem(me // 16 + i, 4) * 16 for i in range(4)]
+    xs = [lax.rem(me // 4 + i, 4) * 4 for i in range(4)]
+    zs = [lax.rem(me + i, 4) for i in range(4)]
 
     def exchange(index):
         src, dst = snd.at[index], rcv.at[index]
-
-        def go(i, carry):
-            d = partner(i)
+        for y, x, z in OFFSETS:
+            d = ys[y] + xs[x] + zs[z]
             pltpu.make_async_remote_copy(
                 src_ref=src.at[d],
                 dst_ref=dst.at[me],
@@ -154,9 +169,6 @@
                 device_id={"rows": d},
                 device_id_type=MESH,
             ).start()
-            return carry
-
-        lax.fori_loop(1, N, go, 0)
         pltpu.make_async_copy(src.at[me], dst.at[me], a_recv.at[index]).start()
 
     def exchange_done(index):
@@ -209,6 +221,9 @@
                     edge = edge + dot(part, place.astype(BF16))
             conv_main[layer, s] = total.astype(BF16)
         conv_edge[layer] = edge.astype(BF16)
+        of = iota((CX, CG), 0) >> 4
+        chosen = jnp.where(of == iota((CX, CG), 1), bias[pl.ds(layer, 1), :], 0.0)
+        bias_col[layer] = jnp.sum(chosen, axis=1, keepdims=True)
 
     def edges_out(layer):
         side = iota((32, CX), 0) >> 4
@@ -222,16 +237,15 @@
             e_snd[layer, 1, :, cols] = rows[CG:]
             return carry
 
-        lax.fori_loop(0, NY // TILE, step, 0)
+        lax.fori_loop(0, TILES, step, 0, unroll=True)
         for copy in edge_copies(layer):
             copy.start()
 
     def shifted(block):
-        wide = block.astype(F32)
-        lane = iota(wide.shape, 1)
-        before = jnp.where(lane == 0, 0.0, pltpu.roll(wide, 1, 1))
-        after = jnp.where(lane == NY - 1, 0.0, pltpu.roll(wide, NY - 1, 1))
-        return before.astype(BF16), after.astype(BF16)
+        zero = jnp.zeros((block.shape[0], 1), BF16)
+        before = jnp.concatenate([zero, block[:, : NY - 1]], axis=1)
+        after = jnp.concatenate([block[:, 1:], zero], axis=1)
+        return before, after
 
     def shift_field():
         def step(i, carry):
@@ -260,10 +274,10 @@
             total += dot(conv_main[layer, 1], h[:, cols])
             total += dot(conv_main[layer, 2], hp[:, cols])
             total += dot(conv_edge[layer], e3[:, cols])
-            acc[:, cols] = total + bias[layer]
+            acc[:, cols] = total + bias_col[layer]
             return carry
 
-        lax.fori_loop(0, NY // TILE, step, 0)
+        lax.fori_loop(0, TILES, step, 0, unroll=True)
 
     def mix(layer):
         blk[...] = rcv[2 * layer].astype(F32).reshape(N * 8, 128)
@@ -358,11 +372,12 @@
         exchange(2 * layer)
         edges_out(layer)
         if layer == 0:
-            for each in range(LAYERS):
-                conv_matrices(each)
+            load_taps.wait()
+            load_bias.wait()
             load_rt.wait()
             load_wt.wait()
         shift_field()
+        conv_matrices(layer)
         exchange_done(2 * layer)
         mix(layer)
         mixed_copy(layer).start()
@@ -386,14 +401,14 @@
                 modes[...] += dot_nt(ft[:, cols], value)
             return carry
 
-        lax.fori_loop(0, NY // TILE, step, 0)
+        lax.fori_loop(0, TILES, step, 0, unroll=True)
 
     def drain(t, carry):
         cols = pl.ds(pl.multiple_of(t * TILE, TILE), TILE)
         pltpu.make_async_copy(h.at[:, cols], out.at[:, cols], o_sem.at[t]).wait()
         return carry
 
-    lax.fori_loop(0, NY // TILE, drain, 0)
+    lax.fori_loop(0, TILES, drain, 0)
     for index in range(2 * LAYERS):
         sent = snd.at[index, pl.ds(0, N - 1)]
         pltpu.make_async_copy(sent, sent, a_send.at[index]).wait()
@@ -403,19 +418,20 @@
     flat = field.reshape(CX, NY)
     weight = spec_weight.reshape(LAYERS, 2, CG, 64, 128)
     taps = conv_weight.reshape(LAYERS, 3, 3, CG, CG)
-    wide_bias = jnp.broadcast_to(bias[:, :, None, None], (LAYERS, CG, XR, 1)).reshape(LAYERS, CX, 1)
     anywhere = pl.BlockSpec(memory_space=pl.ANY)
-    vmem = pl.BlockSpec(memory_space=pltpu.VMEM)
     result = pl.pallas_call(
         kernel,
         out_shape=jax.ShapeDtypeStruct((CX, NY), BF16),
-        in_specs=[anywhere, anywhere, anywhere, anywhere, vmem, vmem],
+        in_specs=[anywhere] * 6,
         out_specs=anywhere,
         scratch_shapes=[
             pltpu.VMEM((CX, NY), BF16),
             pltpu.VMEM((2 * M, NY), BF16),
             pltpu.VMEM((XR * 2 * N, 2 * M), BF16),
             pltpu.VMEM((LAYERS, 2, CG, 64, 128), F32),
+            pltpu.VMEM((LAYERS, 3, 3, CG, CG), BF16),
+            pltpu.VMEM((LAYERS, CG), F32),
+            pltpu.VMEM((LAYERS, CX, 1), F32),
             pltpu.VMEM((CX, NY), BF16),
             pltpu.VMEM((CX, NY), BF16),
             pltpu.VMEM((CX, NY), F32),
@@ -435,14 +451,14 @@
             pltpu.VMEM((LAYERS, 2, CG, NY), BF16),
             pltpu.VMEM((LAYERS, 2, CG, NY), BF16),
             pltpu.VMEM((128, NY), BF16),
-            pltpu.SemaphoreType.DMA((2 * CHUNKS + 2,)),
+            pltpu.SemaphoreType.DMA((2 * CHUNKS + 4,)),
             pltpu.SemaphoreType.DMA((2 * LAYERS,)),
             pltpu.SemaphoreType.DMA((2 * LAYERS,)),
             pltpu.SemaphoreType.DMA((LAYERS,)),
             pltpu.SemaphoreType.DMA((LAYERS,)),
             pltpu.SemaphoreType.DMA((LAYERS, 2)),
             pltpu.SemaphoreType.DMA((LAYERS, 2)),
-            pltpu.SemaphoreType.DMA((NY // TILE,)),
+            pltpu.SemaphoreType.DMA((TILES,)),
         ],
         compiler_params=pltpu.CompilerParams(
             collective_id=0, has_side_effects=True, vmem_limit_bytes=56 * 2**20
@@ -451,7 +467,7 @@
             flops=6 * 10**9, bytes_accessed=10 * 2**20, transcendentals=2 * CX * NY
         ),
         name="fourier_layers",
-    )(flat, jnp.asarray(column_table()), jnp.asarray(row_table()), weight, taps, wide_bias)
+    )(flat, jnp.asarray(column_table()), jnp.asarray(row_table()), weight, taps, bias)
     return result.reshape(CG, XR, NY)
 
 

time: 56.6 us -> 47.5 us (0.84)
  Pallas kernels: 51.6 us -> 44.3 us
  local copies, waits for them, and re-layouts: 4.75 us -> 3.13 us
    pallas_call x1, Pallas kernels: 51.6 us -> 44.3 us  [body(): pl.pallas_call(kernel, out_shape=jax.ShapeDtypeStruct((CX, NY), BF16), in...]
    broadcast_in_dim x2 -> x0, local copies, waits for them, and re-layouts: 1.62 us -> none  [body(): jnp.broadcast_to(bias[:, :, None, None], (LAYERS, CG, XR, 1))]
where the time goes in v2:
time: 47.5 us; the launch traced here: 47.4 us
  Pallas kernels  44.3 us (93%)
  local copies, waits for them, and re-layouts  3.13 us (7%)
    pallas_call x1, Pallas kernels, body(): pl.pallas_call(kernel, out_shape=jax.ShapeDtypeStruct((CX, NY), BF16), in...  44.3 us
    unnamed x1, local copies, waits for them, and re-layouts  3.13 us

profile of v2, /device:TPU:1, one launch (start us, length us, event | category | flops | bytes accessed | tf_op | source)
XLA Modules:
  0.0 47.4 jit_solution(14096072703233109529)
XLA Ops:
  0.0 44.3 %fourier_layers.1 = bf16[256,4096]{1,0:T(8,128)(2,1)} custom-call(bf16[256,4096]{1,0:T(8,128)(2,1)} %bitcast.5, bf16[256,4096]{1,0:T(8,128)(2,1)} %constant.4.clone.table, bf16[2048,256]{1,0:T(8,128)(2,1)} %constant.5.clone.rtable, f32[2,2,16,64,128]{4,3,2,1,0:T(8,128)} %bitcast.6, bf16[2,3,3,16,16]{4,3,2,1,0:T(8,128)(2,1)} %bitcast.7, f32[2,16]{1,0:T(2,128)} %bias_any.1), custom_call_target="tpu_custom_call" | custom-call | flops 6000000000 | bytes 10485760 | tf_op jit(solution)/shard_map/fourier_layers/pallas_call | solution.py:422
  44.3 3.1 %copy.8 = bf16[16,16,4096]{2,1,0:T(8,128)(2,1)} copy(bf16[16,16,4096]{2,1,0:T(8,128)(2,1)} %bitcast.4) | data formatting | bytes 4194304

commit v3 on v2

--- a/solution.py
+++ b/solution.py
@@ -81,9 +81,10 @@
     weight,
     taps_any,
     bias_any,
-    out,
+    acc,
+    ft,
+    spec,
     h,
-    ft,
     rt,
     wt,
     taps,
@@ -91,7 +92,6 @@
     bias_col,
     hm,
     hp,
-    acc,
     modes,
     snd,
     rcv,
@@ -102,7 +102,6 @@
     vs,
     vr,
     vrow,
-    spec,
     conv_main,
     conv_edge,
     e_snd,
@@ -115,7 +114,6 @@
     c_recv,
     e_send,
     e_recv,
-    o_sem,
 ):
     me = lax.axis_index("rows")
     chan = lax.axis_index("chan")
@@ -387,31 +385,32 @@
         convolve(layer)
         exchange_done(2 * layer + 1)
         spectral_rows(layer)
-        last = layer == LAYERS - 1
-        if not last:
+        if layer < LAYERS - 1:
             modes[...] = jnp.zeros_like(modes)
 
-        def step(t, carry):
-            cols = pl.ds(pl.multiple_of(t * TILE, TILE), TILE)
-            value = gelu(acc[:, cols] + dot(spec[...], ft[:, cols])).astype(BF16)
-            h[:, cols] = value
-            if last:
-                pltpu.make_async_copy(h.at[:, cols], out.at[:, cols], o_sem.at[t]).start()
-            else:
+            def step(t, carry):
+                cols = pl.ds(pl.multiple_of(t * TILE, TILE), TILE)
+                value = gelu(acc[:, cols] + dot(spec[...], ft[:, cols])).astype(BF16)
+                h[:, cols] = value
                 modes[...] += dot_nt(ft[:, cols], value)
-            return carry
-
-        lax.fori_loop(0, TILES, step, 0, unroll=True)
-
-    def drain(t, carry):
-        cols = pl.ds(pl.multiple_of(t * TILE, TILE), TILE)
-        pltpu.make_async_copy(h.at[:, cols], out.at[:, cols], o_sem.at[t]).wait()
-        return carry
-
-    lax.fori_loop(0, TILES, drain, 0)
+                return carry
+
+            lax.fori_loop(0, TILES, step, 0, unroll=True)
+
     for index in range(2 * LAYERS):
         sent = snd.at[index, pl.ds(0, N - 1)]
         pltpu.make_async_copy(sent, sent, a_send.at[index]).wait()
+
+
+def finish(acc, ft, spec, out, h, o_sem):
+    copies = []
+    for t in range(TILES):
+        cols = pl.ds(t * TILE, TILE)
+        h[:, cols] = gelu(acc[:, cols] + dot(spec[...], ft[:, cols])).astype(BF16)
+        copies.append(pltpu.make_async_copy(h.at[:, cols], out.at[:, cols], o_sem.at[t]))
+        copies[-1].start()
+    for copy in copies:
+        copy.wait()
 
 
 def body(field, spec_weight, conv_weight, bias):
@@ -419,14 +418,20 @@
     weight = spec_weight.reshape(LAYERS, 2, CG, 64, 128)
     taps = conv_weight.reshape(LAYERS, 3, 3, CG, CG)
     anywhere = pl.BlockSpec(memory_space=pl.ANY)
-    result = pl.pallas_call(
+    operands = [flat, jnp.asarray(column_table()), jnp.asarray(row_table()), weight, taps, bias]
+    operands = [pltpu.with_memory_space_constraint(each, pltpu.HBM) for each in operands]
+    vmem = pl.BlockSpec(memory_space=pltpu.VMEM)
+    acc, ft, spec = pl.pallas_call(
         kernel,
-        out_shape=jax.ShapeDtypeStruct((CX, NY), BF16),
+        out_shape=[
+            pltpu.VMEM((CX, NY), F32),
+            pltpu.VMEM((2 * M, NY), BF16),
+            pltpu.VMEM((CX, 2 * M), BF16),
+        ],
         in_specs=[anywhere] * 6,
-        out_specs=anywhere,
+        out_specs=[vmem] * 3,
         scratch_shapes=[
             pltpu.VMEM((CX, NY), BF16),
-            pltpu.VMEM((2 * M, NY), BF16),
             pltpu.VMEM((XR * 2 * N, 2 * M), BF16),
             pltpu.VMEM((LAYERS, 2, CG, 64, 128), F32),
             pltpu.VMEM((LAYERS, 3, 3, CG, CG), BF16),
@@ -434,7 +439,6 @@
             pltpu.VMEM((LAYERS, CX, 1), F32),
             pltpu.VMEM((CX, NY), BF16),
             pltpu.VMEM((CX, NY), BF16),
-            pltpu.VMEM((CX, NY), F32),
             pltpu.VMEM((2 * M, CX), F32),
             pltpu.VMEM((2 * LAYERS, N, 8, 128), BF16),
             pltpu.VMEM((2 * LAYERS, N, 8, 128), BF16),
@@ -445,7 +449,6 @@
             pltpu.VMEM((LAYERS, 2, 2, 32, 128), F32),
             pltpu.VMEM((LAYERS, 2, 32, 128), F32),
             pltpu.VMEM((2, 32, 128), F32),
-            pltpu.VMEM((CX, 2 * M), BF16),
             pltpu.VMEM((LAYERS, 3, CX, CX), BF16),
             pltpu.VMEM((LAYERS, CX, 128), BF16),
             pltpu.VMEM((LAYERS, 2, CG, NY), BF16),
@@ -458,16 +461,24 @@
             pltpu.SemaphoreType.DMA((LAYERS,)),
             pltpu.SemaphoreType.DMA((LAYERS, 2)),
             pltpu.SemaphoreType.DMA((LAYERS, 2)),
-            pltpu.SemaphoreType.DMA((TILES,)),
         ],
         compiler_params=pltpu.CompilerParams(
-            collective_id=0, has_side_effects=True, vmem_limit_bytes=56 * 2**20
+            collective_id=0, has_side_effects=True, vmem_limit_bytes=40 * 2**20
         ),
         cost_estimate=pl.CostEstimate(
             flops=6 * 10**9, bytes_accessed=10 * 2**20, transcendentals=2 * CX * NY
         ),
         name="fourier_layers",
-    )(flat, jnp.asarray(column_table()), jnp.asarray(row_table()), weight, taps, bias)
+    )(*operands)
+    result = pl.pallas_call(
+        finish,
+        out_shape=jax.ShapeDtypeStruct((CX, NY), BF16),
+        in_specs=[vmem] * 3,
+        out_specs=anywhere,
+        scratch_shapes=[pltpu.VMEM((CX, NY), BF16), pltpu.SemaphoreType.DMA((TILES,))],
+        compiler_params=pltpu.CompilerParams(vmem_limit_bytes=16 * 2**20),
+        name="last_rows",
+    )(acc, ft, spec)
     return result.reshape(CG, XR, NY)
 
 

time: 47.5 us -> 44.5 us (0.937)
  local copies, waits for them, and re-layouts: 3.13 us -> 0 us
    unnamed x1 -> x0, local copies, waits for them, and re-layouts: 3.13 us -> none
    pallas_call x1 -> x2, Pallas kernels: 44.3 us -> 44.3 us  [the longest x1 41.7 us: body(): pl.pallas_call(kernel, out_shape=[pltpu.VMEM((CX, NY), F32), pltpu.VMEM((...]
where the time goes in v3:
time: 44.5 us; the launch traced here: 44.4 us
  Pallas kernels  44.3 us (100%)
    pallas_call x1, Pallas kernels, body(): pl.pallas_call(kernel, out_shape=[pltpu.VMEM((CX, NY), F32), pltpu.VMEM((...  41.7 us
    pallas_call x1, Pallas kernels, body(): pl.pallas_call(finish, out_shape=jax.ShapeDtypeStruct((CX, NY), BF16), in...  2.58 us

profile of v3, /device:TPU:1, one launch (start us, length us, event | category | flops | bytes accessed | tf_op | source)
XLA Modules:
  0.0 44.4 jit_solution(4883345247802798506)
XLA Ops:
  0.0 41.7 %fourier_layers.1 = (f32[256,4096]{1,0:T(8,128)S(1)}, bf16[256,4096]{1,0:T(8,128)(2,1)S(1)}, bf16[256,256]{1,0:T(8,128)(2,1)S(1)}) custom-call(bf16[256,4096]{1,0:T(8,128)(2,1)} %bitcast.4, bf16[256,4096]{1,0:T(8,128)(2,1)} %constant.4.clone.table, bf16[2048,256]{1,0:T(8,128)(2,1)} %constant.5.clone.rtable, f32[2,2,16,64,128]{4,3,2,1,0:T(8,128)} %bitcast.5, ...), custom_call_target="tpu_custom_call" | custom-call | flops 6000000000 | bytes 10485760 | tf_op jit(solution)/shard_map/fourier_layers/pallas_call | solution.py:424
  41.7 2.6 %last_rows.1 = bf16[256,4096]{1,0:T(8,128)(2,1)} custom-call(f32[256,4096]{1,0:T(8,128)S(1)} %get-tuple-element.8.acc, bf16[256,4096]{1,0:T(8,128)(2,1)S(1)} %get-tuple-element.9.ft, bf16[256,256]{1,0:T(8,128)(2,1)S(1)} %get-tuple-element.10.spec), custom_call_target="tpu_custom_call" | custom-call | tf_op jit(solution)/shard_map/last_rows/pallas_call | solution.py:473

commit v4 on v3

--- a/solution.py
+++ b/solution.py
@@ -20,6 +20,8 @@
 CX = CG * XR
 TILE = 1024
 TILES = NY // TILE
+PIECE = 512
+PIECES = NY // PIECE
 CHUNKS = 4
 F32 = jnp.float32
 BF16 = jnp.bfloat16
@@ -67,7 +69,8 @@
 
 
 def gelu(v):
-    return 0.5 * v * (1.0 + jnp.tanh(0.7978845608 * (v + 0.044715 * (v * v * v))))
+    half = 0.5 * v
+    return half + half * jnp.tanh(v * (0.7978845608 + (0.7978845608 * 0.044715) * (v * v)))
 
 
 def iota(shape, dim):
@@ -78,6 +81,7 @@
     field,
     table,
     rtable,
+    btable,
     weight,
     taps_any,
     bias_any,
@@ -86,6 +90,7 @@
     spec,
     h,
     rt,
+    bt,
     wt,
     taps,
     bias,
@@ -129,6 +134,7 @@
             )
         )
     load_rt = pltpu.make_async_copy(rtable, rt, ld_sem.at[2 * CHUNKS])
+    load_bt = pltpu.make_async_copy(btable, bt, ld_sem.at[2 * CHUNKS + 4])
     load_wt = pltpu.make_async_copy(weight, wt, ld_sem.at[2 * CHUNKS + 1])
     load_taps = pltpu.make_async_copy(taps_any, taps, ld_sem.at[2 * CHUNKS + 2])
     load_bias = pltpu.make_async_copy(bias_any, bias, ld_sem.at[2 * CHUNKS + 3])
@@ -139,6 +145,7 @@
     load_bias.start()
     load_rt.start()
     load_wt.start()
+    load_bt.start()
 
     barrier = pltpu.get_barrier_semaphore()
 
@@ -288,27 +295,38 @@
             lhs[:, pl.ds(x * 128, 128)] = jnp.concatenate(rows, axis=0).astype(BF16)
         usc[...] = dot(lhs[...], rt[...])
         odd = (iota((8, 128), 0) & 1) == 1
-        real = jnp.zeros((8, 8, 128), F32)
-        imag = jnp.zeros((8, 8, 128), F32)
+        values = []
         for c in range(CG):
-            ur, ui = [
-                jnp.where(
-                    odd,
-                    jnp.broadcast_to(usc[pl.ds(CG + c, 1), pl.ds(p * 128, 128)], (8, 128)),
-                    jnp.broadcast_to(usc[pl.ds(c, 1), pl.ds(p * 128, 128)], (8, 128)),
-                )[None]
-                for p in range(2)
-            ]
-            wr = wt[layer, 0, c].reshape(8, 8, 128)
-            wi = wt[layer, 1, c].reshape(8, 8, 128)
-            real += wr * ur - wi * ui
-            imag += wr * ui + wi * ur
-        vs[layer, :, 0] = real.reshape(2, 32, 128)
-        vs[layer, :, 1] = imag.reshape(2, 32, 128)
+            values.append(
+                [
+                    jnp.where(
+                        odd,
+                        jnp.broadcast_to(usc[pl.ds(CG + c, 1), pl.ds(p * 128, 128)], (8, 128)),
+                        jnp.broadcast_to(usc[pl.ds(c, 1), pl.ds(p * 128, 128)], (8, 128)),
+                    )[None]
+                    for p in range(2)
+                ]
+            )
+
+        def half_of(part):
+            rows = pl.ds(pl.multiple_of(part * 32, 32), 32)
+            real = jnp.zeros((4, 8, 128), F32)
+            imag = jnp.zeros((4, 8, 128), F32)
+            for c in range(CG):
+                ur, ui = values[c]
+                wr = wt[layer, 0, c, rows, :].reshape(4, 8, 128)
+                wi = wt[layer, 1, c, rows, :].reshape(4, 8, 128)
+                real += wr * ur - wi * ui
+                imag += wr * ui + wi * ur
+            return real.reshape(32, 128), imag.reshape(32, 128)
+
+        vs[layer, 0], vs[layer, 1] = half_of(1 - chan)
+        mixed_copy(layer).start()
+        vrow[0], vrow[1] = half_of(chan)
 
     def mixed_copy(layer):
         return pltpu.make_async_remote_copy(
-            src_ref=vs.at[layer, 1 - chan],
+            src_ref=vs.at[layer],
             dst_ref=vr.at[layer],
             send_sem=c_send.at[layer],
             recv_sem=c_recv.at[layer],
@@ -317,7 +335,7 @@
         )
 
     def back_rows(layer):
-        vrow[...] = vs[layer, chan] + vr[layer]
+        vrow[...] += vr[layer]
         mixed = jnp.concatenate(
             [
                 jnp.concatenate([vrow[p, pl.ds(kk, CG, stride=2), :] for kk in range(2)], axis=0)
@@ -325,8 +343,9 @@
             ],
             axis=1,
         ).astype(BF16)
+        product = dot(mixed, bt[...])
         for x in range(XR):
-            piece = dot_nt(mixed, rt[pl.ds(x * 128, 128), :])
+            piece = product[:, x * 128 : x * 128 + 128]
             for i in range(4):
                 ysc[i, pl.ds(x, 8, stride=XR), :] = piece[8 * i : 8 * i + 8]
         scale = 2.0 / (M * math.sqrt(NX * NY))
@@ -374,11 +393,11 @@
             load_bias.wait()
             load_rt.wait()
             load_wt.wait()
+            load_bt.wait()
         shift_field()
         conv_matrices(layer)
         exchange_done(2 * layer)
         mix(layer)
-        mixed_copy(layer).start()
         mixed_copy(layer).wait()
         back_rows(layer)
         exchange(2 * layer + 1)
@@ -388,25 +407,29 @@
         if layer < LAYERS - 1:
             modes[...] = jnp.zeros_like(modes)
 
-            def step(t, carry):
-                cols = pl.ds(pl.multiple_of(t * TILE, TILE), TILE)
-                value = gelu(acc[:, cols] + dot(spec[...], ft[:, cols])).astype(BF16)
+            for t, cols, product in column_pieces(spec, ft):
+                value = gelu(acc[:, cols] + product).astype(BF16)
                 h[:, cols] = value
                 modes[...] += dot_nt(ft[:, cols], value)
-                return carry
-
-            lax.fori_loop(0, TILES, step, 0, unroll=True)
 
     for index in range(2 * LAYERS):
         sent = snd.at[index, pl.ds(0, N - 1)]
         pltpu.make_async_copy(sent, sent, a_send.at[index]).wait()
 
 
+def column_pieces(spec, ft):
+    ahead = dot(spec[...], ft[:, pl.ds(0, PIECE)])
+    for t in range(PIECES):
+        now = ahead
+        if t + 1 < PIECES:
+            ahead = dot(spec[...], ft[:, pl.ds((t + 1) * PIECE, PIECE)])
+        yield t, pl.ds(t * PIECE, PIECE), now
+
+
 def finish(acc, ft, spec, out, h, o_sem):
     copies = []
-    for t in range(TILES):
-        cols = pl.ds(t * TILE, TILE)
-        h[:, cols] = gelu(acc[:, cols] + dot(spec[...], ft[:, cols])).astype(BF16)
+    for t, cols, product in column_pieces(spec, ft):
+        h[:, cols] = gelu(acc[:, cols] + product).astype(BF16)
         copies.append(pltpu.make_async_copy(h.at[:, cols], out.at[:, cols], o_sem.at[t]))
         copies[-1].start()
     for copy in copies:
@@ -418,7 +441,9 @@
     weight = spec_weight.reshape(LAYERS, 2, CG, 64, 128)
     taps = conv_weight.reshape(LAYERS, 3, 3, CG, CG)
     anywhere = pl.BlockSpec(memory_space=pl.ANY)
-    operands = [flat, jnp.asarray(column_table()), jnp.asarray(row_table()), weight, taps, bias]
+    rows = row_table()
+    tables = [jnp.asarray(each) for each in (column_table(), rows, np.ascontiguousarray(rows.T))]
+    operands = [flat, *tables, weight, taps, bias]
     operands = [pltpu.with_memory_space_constraint(each, pltpu.HBM) for each in operands]
     vmem = pl.BlockSpec(memory_space=pltpu.VMEM)
     acc, ft, spec = pl.pallas_call(
@@ -428,11 +453,12 @@
             pltpu.VMEM((2 * M, NY), BF16),
             pltpu.VMEM((CX, 2 * M), BF16),
         ],
-        in_specs=[anywhere] * 6,
+        in_specs=[anywhere] * 7,
         out_specs=[vmem] * 3,
         scratch_shapes=[
             pltpu.VMEM((CX, NY), BF16),
             pltpu.VMEM((XR * 2 * N, 2 * M), BF16),
+            pltpu.VMEM((2 * M, XR * 2 * N), BF16),
             pltpu.VMEM((LAYERS, 2, CG, 64, 128), F32),
             pltpu.VMEM((LAYERS, 3, 3, CG, CG), BF16),
             pltpu.VMEM((LAYERS, CG), F32),
@@ -446,7 +472,7 @@
             pltpu.VMEM((4, 128, 128), F32),
             pltpu.VMEM((32, XR * 128), BF16),
             pltpu.VMEM((32, 256), F32),
-            pltpu.VMEM((LAYERS, 2, 2, 32, 128), F32),
+            pltpu.VMEM((LAYERS, 2, 32, 128), F32),
             pltpu.VMEM((LAYERS, 2, 32, 128), F32),
             pltpu.VMEM((2, 32, 128), F32),
             pltpu.VMEM((LAYERS, 3, CX, CX), BF16),
@@ -454,7 +480,7 @@
             pltpu.VMEM((LAYERS, 2, CG, NY), BF16),
             pltpu.VMEM((LAYERS, 2, CG, NY), BF16),
             pltpu.VMEM((128, NY), BF16),
-            pltpu.SemaphoreType.DMA((2 * CHUNKS + 4,)),
+            pltpu.SemaphoreType.DMA((2 * CHUNKS + 5,)),
             pltpu.SemaphoreType.DMA((2 * LAYERS,)),
             pltpu.SemaphoreType.DMA((2 * LAYERS,)),
             pltpu.SemaphoreType.DMA((LAYERS,)),
@@ -475,7 +501,7 @@
         out_shape=jax.ShapeDtypeStruct((CX, NY), BF16),
         in_specs=[vmem] * 3,
         out_specs=anywhere,
-        scratch_shapes=[pltpu.VMEM((CX, NY), BF16), pltpu.SemaphoreType.DMA((TILES,))],
+        scratch_shapes=[pltpu.VMEM((CX, NY), BF16), pltpu.SemaphoreType.DMA((PIECES,))],
         compiler_params=pltpu.CompilerParams(vmem_limit_bytes=16 * 2**20),
         name="last_rows",
     )(acc, ft, spec)

time: 44.5 us -> 43.8 us (0.984)
  Pallas kernels: 44.3 us -> 43.6 us
    pallas_call x1, Pallas kernels: 41.7 us -> 41.1 us  [body(): pl.pallas_call(kernel, out_shape=[pltpu.VMEM((CX, NY), F32), pltpu.VMEM((...]
where the time goes in v4:
time: 43.8 us; the launch traced here: 43.7 us
  Pallas kernels  43.6 us (100%)
    pallas_call x1, Pallas kernels, body(): pl.pallas_call(kernel, out_shape=[pltpu.VMEM((CX, NY), F32), pltpu.VMEM((...  41.1 us
    pallas_call x1, Pallas kernels, body(): pl.pallas_call(finish, out_shape=jax.ShapeDtypeStruct((CX, NY), BF16), in...  2.46 us

profile of v4, /device:TPU:1, one launch (start us, length us, event | category | flops | bytes accessed | tf_op | source)
XLA Modules:
  0.0 43.7 jit_solution(9108549844062209010)
XLA Ops:
  0.0 41.1 %fourier_layers.1 = (f32[256,4096]{1,0:T(8,128)S(1)}, bf16[256,4096]{1,0:T(8,128)(2,1)S(1)}, bf16[256,256]{1,0:T(8,128)(2,1)S(1)}) custom-call(bf16[256,4096]{1,0:T(8,128)(2,1)} %bitcast.4, bf16[256,4096]{1,0:T(8,128)(2,1)} %constant.6.clone.table, bf16[2048,256]{1,0:T(8,128)(2,1)} %constant.7.clone.rtable, bf16[256,2048]{1,0:T(8,128)(2,1)} %constant.8.clone.btable, ...), custom_call_target="tpu_custom_call" | custom-call | flops 6000000000 | bytes 10485760 | tf_op jit(solution)/shard_map/fourier_layers/pallas_call | solution.py:449
  41.1 2.5 %last_rows.1 = bf16[256,4096]{1,0:T(8,128)(2,1)} custom-call(f32[256,4096]{1,0:T(8,128)S(1)} %get-tuple-element.8.acc, bf16[256,4096]{1,0:T(8,128)(2,1)S(1)} %get-tuple-element.9.ft, bf16[256,256]{1,0:T(8,128)(2,1)S(1)} %get-tuple-element.10.spec), custom_call_target="tpu_custom_call" | custom-call | tf_op jit(solution)/shard_map/last_rows/pallas_call | solution.py:499

commit v5 on v4

--- a/solution.py
+++ b/solution.py
@@ -68,9 +68,9 @@
     return lax.dot_general(a, b, (((1,), (1,)), ((), ())), preferred_element_type=F32)
 
 
-def gelu(v):
-    half = 0.5 * v
-    return half + half * jnp.tanh(v * (0.7978845608 + (0.7978845608 * 0.044715) * (v * v)))
+def gelu_of_half(w):
+    inner = w * (2.0 * 0.7978845608 + (8.0 * 0.7978845608 * 0.044715) * (w * w))
+    return w + w * jnp.tanh(inner)
 
 
 def iota(shape, dim):
@@ -123,6 +123,18 @@
     me = lax.axis_index("rows")
     chan = lax.axis_index("chan")
     width = NY // CHUNKS
+    barrier = pltpu.get_barrier_semaphore()
+    ys = [lax.rem(me // 16 + i, 4) * 16 for i in range(4)]
+    xs = [lax.rem(me // 4 + i, 4) * 4 for i in range(4)]
+    zs = [lax.rem(me + i, 4) for i in range(4)]
+
+    def greet(offsets):
+        for y, x, z in offsets:
+            pl.semaphore_signal(
+                barrier, inc=1, device_id={"rows": ys[y] + xs[x] + zs[z]}, device_id_type=MESH
+            )
+
+    greet(OFFSETS[:7])
 
     loads = []
     for i in range(CHUNKS):
@@ -141,26 +153,14 @@
     for one, two in loads:
         one.start()
         two.start()
+    greet(OFFSETS[7:])
+    pl.semaphore_signal(barrier, inc=1, device_id={"chan": 1 - chan}, device_id_type=MESH)
     load_taps.start()
     load_bias.start()
     load_rt.start()
     load_wt.start()
     load_bt.start()
 
-    barrier = pltpu.get_barrier_semaphore()
-
-    def greet(i, carry):
-        pl.semaphore_signal(
-            barrier, inc=1, device_id={"rows": lax.rem(me + i, N)}, device_id_type=MESH
-        )
-        return carry
-
-    lax.fori_loop(1, N, greet, 0)
-    pl.semaphore_signal(barrier, inc=1, device_id={"chan": 1 - chan}, device_id_type=MESH)
-
-    ys = [lax.rem(me // 16 + i, 4) * 16 for i in range(4)]
-    xs = [lax.rem(me // 4 + i, 4) * 4 for i in range(4)]
-    zs = [lax.rem(me + i, 4) for i in range(4)]
 
     def exchange(index):
         src, dst = snd.at[index], rcv.at[index]
@@ -224,11 +224,11 @@
                     place = (iota((CG, 128), 1) == iota((CG, 128), 0) + offset).astype(F32)
                     part = jnp.where(xr == keep, tap, 0.0).astype(BF16)
                     edge = edge + dot(part, place.astype(BF16))
-            conv_main[layer, s] = total.astype(BF16)
-        conv_edge[layer] = edge.astype(BF16)
+            conv_main[layer, s] = (0.5 * total).astype(BF16)
+        conv_edge[layer] = (0.5 * edge).astype(BF16)
         of = iota((CX, CG), 0) >> 4
         chosen = jnp.where(of == iota((CX, CG), 1), bias[pl.ds(layer, 1), :], 0.0)
-        bias_col[layer] = jnp.sum(chosen, axis=1, keepdims=True)
+        bias_col[layer] = 0.5 * jnp.sum(chosen, axis=1, keepdims=True)
 
     def edges_out(layer):
         side = iota((32, CX), 0) >> 4
@@ -262,7 +262,7 @@
 
         lax.fori_loop(0, CX // 16, step, 0)
 
-    def convolve(layer):
+    def edges_in(layer):
         for copy in edge_copies(layer):
             copy.wait()
         for side in range(2):
@@ -273,16 +273,17 @@
             e3[pl.ds(64 + side * CG, CG), :] = after
         e3[pl.ds(96, 32), :] = jnp.zeros((32, NY), BF16)
 
-        def step(t, carry):
-            cols = pl.ds(pl.multiple_of(t * TILE, TILE), TILE)
-            total = dot(conv_main[layer, 0], hm[:, cols])
-            total += dot(conv_main[layer, 1], h[:, cols])
-            total += dot(conv_main[layer, 2], hp[:, cols])
-            total += dot(conv_edge[layer], e3[:, cols])
-            acc[:, cols] = total + bias_col[layer]
-            return carry
-
-        lax.fori_loop(0, TILES, step, 0, unroll=True)
+    def convolve(layer, tiles, main=True, edge=True):
+        for t in tiles:
+            cols = pl.ds(t * TILE, TILE)
+            total = bias_col[layer] if main else acc[:, cols]
+            if main:
+                total = total + dot(conv_main[layer, 0], hm[:, cols])
+                total += dot(conv_main[layer, 1], h[:, cols])
+                total += dot(conv_main[layer, 2], hp[:, cols])
+            if edge:
+                total += dot(conv_edge[layer], e3[:, cols])
+            acc[:, cols] = total
 
     def mix(layer):
         blk[...] = rcv[2 * layer].astype(F32).reshape(N * 8, 128)
@@ -348,7 +349,7 @@
             piece = product[:, x * 128 : x * 128 + 128]
             for i in range(4):
                 ysc[i, pl.ds(x, 8, stride=XR), :] = piece[8 * i : 8 * i + 8]
-        scale = 2.0 / (M * math.sqrt(NX * NY))
+        scale = 1.0 / (M * math.sqrt(NX * NY))
         for kk in range(2):
             first = jnp.where(me == 0, 0.5 * scale, scale) if kk == 0 else scale
             for half in range(2):
@@ -385,30 +386,35 @@
     for layer in range(LAYERS):
         forward_send(layer)
         if layer == 0:
+            load_taps.wait()
+            load_bias.wait()
+            conv_matrices(0)
             pl.semaphore_wait(barrier, N)
         exchange(2 * layer)
         edges_out(layer)
         if layer == 0:
-            load_taps.wait()
-            load_bias.wait()
             load_rt.wait()
             load_wt.wait()
             load_bt.wait()
         shift_field()
-        conv_matrices(layer)
+        if layer == 0:
+            conv_matrices(1)
+        convolve(layer, range(1), edge=False)
         exchange_done(2 * layer)
         mix(layer)
         mixed_copy(layer).wait()
         back_rows(layer)
         exchange(2 * layer + 1)
-        convolve(layer)
+        edges_in(layer)
+        convolve(layer, range(1), main=False)
+        convolve(layer, range(1, TILES))
         exchange_done(2 * layer + 1)
         spectral_rows(layer)
         if layer < LAYERS - 1:
             modes[...] = jnp.zeros_like(modes)
 
             for t, cols, product in column_pieces(spec, ft):
-                value = gelu(acc[:, cols] + product).astype(BF16)
+                value = gelu_of_half(acc[:, cols] + product).astype(BF16)
                 h[:, cols] = value
                 modes[...] += dot_nt(ft[:, cols], value)
 
@@ -429,7 +435,7 @@
 def finish(acc, ft, spec, out, h, o_sem):
     copies = []
     for t, cols, product in column_pieces(spec, ft):
-        h[:, cols] = gelu(acc[:, cols] + product).astype(BF16)
+        h[:, cols] = gelu_of_half(acc[:, cols] + product).astype(BF16)
         copies.append(pltpu.make_async_copy(h.at[:, cols], out.at[:, cols], o_sem.at[t]))
         copies[-1].start()
     for copy in copies:

time: 43.8 us -> 42.7 us (0.975)
  Pallas kernels: 43.6 us -> 42.4 us
    pallas_call x1, Pallas kernels: 41.1 us -> 40.1 us  [body(): pl.pallas_call(kernel, out_shape=[pltpu.VMEM((CX, NY), F32), pltpu.VMEM((...]
where the time goes in v5:
time: 42.7 us; the launch traced here: 42.6 us
  Pallas kernels  42.4 us (99%)
    pallas_call x1, Pallas kernels, body(): pl.pallas_call(kernel, out_shape=[pltpu.VMEM((CX, NY), F32), pltpu.VMEM((...  40.1 us
    pallas_call x1, Pallas kernels, body(): pl.pallas_call(finish, out_shape=jax.ShapeDtypeStruct((CX, NY), BF16), in...  2.28 us

profile of v5, /device:TPU:1, one launch (start us, length us, event | category | flops | bytes accessed | tf_op | source)
XLA Modules:
  0.0 42.6 jit_solution(1384279177721461917)
XLA Ops:
  0.0 40.1 %fourier_layers.1 = (f32[256,4096]{1,0:T(8,128)S(1)}, bf16[256,4096]{1,0:T(8,128)(2,1)S(1)}, bf16[256,256]{1,0:T(8,128)(2,1)S(1)}) custom-call(bf16[256,4096]{1,0:T(8,128)(2,1)} %bitcast.4, bf16[256,4096]{1,0:T(8,128)(2,1)} %constant.6.clone.table, bf16[2048,256]{1,0:T(8,128)(2,1)} %constant.7.clone.rtable, bf16[256,2048]{1,0:T(8,128)(2,1)} %constant.8.clone.btable, ...), custom_call_target="tpu_custom_call" | custom-call | flops 6000000000 | bytes 10485760 | tf_op jit(solution)/shard_map/fourier_layers/pallas_call | solution.py:455
  40.1 2.3 %last_rows.1 = bf16[256,4096]{1,0:T(8,128)(2,1)} custom-call(f32[256,4096]{1,0:T(8,128)S(1)} %get-tuple-element.8.acc, bf16[256,4096]{1,0:T(8,128)(2,1)S(1)} %get-tuple-element.9.ft, bf16[256,256]{1,0:T(8,128)(2,1)S(1)} %get-tuple-element.10.spec), custom_call_target="tpu_custom_call" | custom-call | tf_op jit(solution)/shard_map/last_rows/pallas_call | solution.py:505

commit v6 on v5

--- a/solution.py
+++ b/solution.py
@@ -383,22 +383,24 @@
         loads[i][1].wait()
         modes[...] += dot_nt(ft[:, cols], h[:, cols])
 
-    for layer in range(LAYERS):
+    load_taps.wait()
+    load_bias.wait()
+    conv_matrices(0)
+    pl.semaphore_wait(barrier, N)
+
+    def one_layer(layer, carry):
         forward_send(layer)
-        if layer == 0:
-            load_taps.wait()
-            load_bias.wait()
-            conv_matrices(0)
-            pl.semaphore_wait(barrier, N)
         exchange(2 * layer)
         edges_out(layer)
-        if layer == 0:
+        shift_field()
+
+        @pl.when(layer == 0)
+        def _():
             load_rt.wait()
             load_wt.wait()
             load_bt.wait()
-        shift_field()
-        if layer == 0:
             conv_matrices(1)
+
         convolve(layer, range(1), edge=False)
         exchange_done(2 * layer)
         mix(layer)
@@ -410,14 +412,19 @@
         convolve(layer, range(1, TILES))
         exchange_done(2 * layer + 1)
         spectral_rows(layer)
-        if layer < LAYERS - 1:
+
+        @pl.when(layer < LAYERS - 1)
+        def _():
             modes[...] = jnp.zeros_like(modes)
-
             for t, cols, product in column_pieces(spec, ft):
-                value = gelu_of_half(acc[:, cols] + product).astype(BF16)
-                h[:, cols] = value
-                modes[...] += dot_nt(ft[:, cols], value)
-
+                h[:, cols] = gelu_of_half(acc[:, cols] + product).astype(BF16)
+                if t % 4 == 3:
+                    done = pl.ds((t - 3) * PIECE, 4 * PIECE)
+                    modes[...] += dot_nt(ft[:, done], h[:, done])
+
+        return carry
+
+    lax.fori_loop(0, LAYERS, one_layer, 0)
     for index in range(2 * LAYERS):
         sent = snd.at[index, pl.ds(0, N - 1)]
         pltpu.make_async_copy(sent, sent, a_send.at[index]).wait()

time: 42.7 us -> 42.4 us (level)
  no operation moved by 1% of the time
where the time goes in v6:
time: 42.4 us; the launch traced here: 42.3 us
  Pallas kernels  42.3 us (100%)
    pallas_call x1, Pallas kernels, body(): pl.pallas_call(kernel, out_shape=[pltpu.VMEM((CX, NY), F32), pltpu.VMEM((...  40 us
    pallas_call x1, Pallas kernels, body(): pl.pallas_call(finish, out_shape=jax.ShapeDtypeStruct((CX, NY), BF16), in...  2.27 us

profile of v6, /device:TPU:1, one launch (start us, length us, event | category | flops | bytes accessed | tf_op | source)
XLA Modules:
  0.0 42.3 jit_solution(8795053298605330735)
XLA Ops:
  0.0 40.0 %fourier_layers.1 = (f32[256,4096]{1,0:T(8,128)S(1)}, bf16[256,4096]{1,0:T(8,128)(2,1)S(1)}, bf16[256,256]{1,0:T(8,128)(2,1)S(1)}) custom-call(bf16[256,4096]{1,0:T(8,128)(2,1)} %bitcast.4, bf16[256,4096]{1,0:T(8,128)(2,1)} %constant.6.clone.table, bf16[2048,256]{1,0:T(8,128)(2,1)} %constant.7.clone.rtable, bf16[256,2048]{1,0:T(8,128)(2,1)} %constant.8.clone.btable, ...), custom_call_target="tpu_custom_call" | custom-call | flops 6000000000 | bytes 10485760 | tf_op jit(solution)/shard_map/fourier_layers/pallas_call | solution.py:462
  40.0 2.3 %last_rows.1 = bf16[256,4096]{1,0:T(8,128)(2,1)} custom-call(f32[256,4096]{1,0:T(8,128)S(1)} %get-tuple-element.8.acc, bf16[256,4096]{1,0:T(8,128)(2,1)S(1)} %get-tuple-element.9.ft, bf16[256,256]{1,0:T(8,128)(2,1)S(1)} %get-tuple-element.10.spec), custom_call_target="tpu_custom_call" | custom-call | tf_op jit(solution)/shard_map/last_rows/pallas_call | solution.py:512
